TPU v7x, 32 devices: a whole 2x2x4 slice. The times are simulated.
32 devices in a mesh: section: 4 (over y, x), expert: 8 (over z, core).
Axes of the slice: x: 2, y: 2, z: 4, core: 2. Of those that a mesh axis runs over, the one named last changes fastest.
Arguments:
- hidden: bfloat16 [4, 512, 4096], P('section', 'expert'), may hold values from -6 to 6
- queries: bfloat16 [4, 512, 4096], P('section', 'expert'), may hold values from -10 to 10
- fresh_kv: bfloat16 [4, 2, 512, 256], P('section', None, 'expert'), may hold values from -10 to 10
- cache_kv: bfloat16 [4, 2, 256, 256], P('section', None, 'expert'), may hold values from -10 to 10
- cache_fill: int32 [4], P('section'), may hold values from 128 to 256, as said below
- out_proj: bfloat16 [4, 4096, 4096], P('section', 'expert'), may hold values from -0.375 to 0.375
- norm_gain: bfloat16 [4, 4096], P('section'), may hold values from 0.5 to 1.5
- router_weight: bfloat16 [4, 4096, 128], P('section'), may hold values from -3 to 3
- expert_labels: int32 [4, 512, 8], P('section', 'expert'), may hold values from 0 to 127, as said below
- gate_proj: bfloat16 [4, 8, 4096, 384], P('section', 'expert'), may hold values from -0.09375 to 0.09375
- up_proj: bfloat16 [4, 8, 4096, 384], P('section', 'expert'), may hold values from -0.09375 to 0.09375
- down_proj: bfloat16 [4, 8, 384, 4096], P('section', 'expert'), may hold values from -0.15625 to 0.15625
Outputs:
- passed: bfloat16 [4, 512, 4096], P('section', 'expert')
Inputs may be any that keep to these rules, and one draw needn't show every extreme that they name: `expert_labels`: each row names 8 different experts, exactly one of them below 2. At most 56 of the 64 tokens of one device name one expert below 2, and on every device some expert is named by 56 of them. `cache_fill`: at least 128; some section has 256.
All inputs are finite; a program needn't handle non-finite values.
Results may differ from a plain program's by a relative error of at most 0.008.
Values may be sent and summed in bfloat16 or wider, within the bound.
A program may use at most 256 MiB of HBM per device.

v0:
```python
import math

import jax
import jax.numpy as jnp
from jax import lax
from jax.sharding import PartitionSpec as P

D = 4096
QUERY_HEADS = 32
KEY_VALUE_HEADS = 2
HEAD_SIZE = 128
EXPERTS = 128
SPLIT = 4


def shifted(shard, axis, by):
    length = lax.axis_size(axis)
    return lax.ppermute(shard, axis, [(i, (i + by) % length) for i in range(length)])


def shards(
    hidden,
    queries,
    fresh_kv,
    cache_kv,
    cache_fill,
    out_proj,
    norm_gain,
    router_weight,
    expert_labels,
    gate_proj,
    up_proj,
    down_proj,
):
    devices = lax.axis_size("expert")
    device_index = lax.axis_index("expert")
    section_tokens = hidden.shape[1]
    local_cache = cache_kv.shape[2]
    stride = local_cache + section_tokens
    head_group = QUERY_HEADS // KEY_VALUE_HEADS
    scale = 1.0 / math.sqrt(HEAD_SIZE)
    fill = cache_fill[0]
    query_pos = device_index * section_tokens + jnp.arange(section_tokens, dtype=jnp.int32)
    gathered_queries = queries[0].reshape(section_tokens, KEY_VALUE_HEADS, head_group, HEAD_SIZE)
    joined_rows = jnp.concatenate([cache_kv[0], fresh_kv[0]], axis=1)

    def attend_block(carry, block_key_value, start):
        run_max, run_sum, run_acc = carry
        token_count = block_key_value.shape[1]
        row_index = start + jnp.arange(token_count, dtype=jnp.int32)
        owner = row_index // stride
        offset = row_index % stride
        cache_pos = owner * local_cache + offset
        slice_pos = owner * section_tokens + offset - local_cache
        visible = jnp.where(
            offset[None, :] < local_cache,
            cache_pos[None, :] < fill,
            slice_pos[None, :] <= query_pos[:, None],
        )
        key_matrix = block_key_value[0].reshape(token_count, KEY_VALUE_HEADS, HEAD_SIZE)
        value_matrix = block_key_value[1].reshape(token_count, KEY_VALUE_HEADS, HEAD_SIZE)
        scores = (
            jnp.einsum(
                "tgkd,rgd->tgkr", gathered_queries, key_matrix, preferred_element_type=jnp.float32
            )
            * scale
        )
        mask = visible[:, None, None, :]
        masked = jnp.where(mask, scores, -1e30)
        new_max = jnp.maximum(run_max, jnp.max(masked, axis=3))
        weights = jnp.where(mask, jnp.exp(masked - new_max[..., None]), 0.0)
        factor = jnp.exp(run_max - new_max)
        new_sum = run_sum * factor + jnp.sum(weights, axis=3)
        rounded = weights.astype(jnp.bfloat16)
        new_acc = run_acc * factor[..., None] + jnp.einsum(
            "tgkr,rgd->tgkd", rounded, value_matrix, preferred_element_type=jnp.float32
        )
        return (new_max, new_sum, new_acc)

    def attend_piece(carry, piece, start):
        token_count = piece.shape[1]
        cache_block = token_count
        while cache_block > 1024 and cache_block % 2 == 0:
            cache_block = cache_block // 2
        relay_steps = token_count // cache_block
        if relay_steps == 1:
            return attend_block(carry, piece, start)
        cache_blocks = jnp.transpose(
            piece.reshape(2, relay_steps, cache_block, KEY_VALUE_HEADS * HEAD_SIZE), (1, 0, 2, 3)
        )
        offsets = start + jnp.arange(relay_steps, dtype=jnp.int32) * cache_block

        def one_step(state, item):
            block_key_value, first = item
            return (attend_block(state, block_key_value, first), None)

        final, unused = lax.scan(one_step, carry, (cache_blocks, offsets))
        return final

    initial_maximum = jnp.full((section_tokens, KEY_VALUE_HEADS, head_group), -1e30, jnp.float32)
    initial_sum = jnp.zeros((section_tokens, KEY_VALUE_HEADS, head_group), jnp.float32)
    initial_accumulator = jnp.zeros(
        (section_tokens, KEY_VALUE_HEADS, head_group, HEAD_SIZE), jnp.float32
    )
    every_key_value = lax.all_gather(joined_rows, "expert", axis=1, tiled=True)
    final_max, final_sum, final_acc = attend_piece(
        (initial_maximum, initial_sum, initial_accumulator), every_key_value, jnp.int32(0)
    )
    attended = (
        (final_acc / final_sum[..., None])
        .reshape(section_tokens, QUERY_HEADS * HEAD_SIZE)
        .astype(jnp.bfloat16)
    )
    projected = jnp.dot(
        attended,
        lax.all_gather(out_proj[0], "expert", axis=0, tiled=True),
        preferred_element_type=jnp.float32,
    )
    mixed = hidden[0].astype(jnp.float32) + projected
    inverse = lax.rsqrt(jnp.mean(mixed * mixed, axis=1, keepdims=True) + 1e-06)
    normed = (mixed * inverse * norm_gain[0].astype(jnp.float32)[None, :]).astype(jnp.bfloat16)
    logits = jnp.dot(normed, router_weight[0], preferred_element_type=jnp.float32)
    label_rows = expert_labels[0]
    matches = label_rows[:, :, None] == jnp.arange(EXPERTS, dtype=jnp.int32)[None, None, :]
    picked = jnp.sum(jnp.where(matches, logits[:, None, :], 0.0), axis=2)
    probabilities = jax.nn.softmax(picked, axis=1)
    airborne_expert = devices // SPLIT
    hot_rows = SPLIT * max(1, section_tokens // (8 * SPLIT))
    other_rows = (section_tokens - hot_rows + airborne_expert - 2) // (airborne_expert - 1)
    capacity = SPLIT * ((max(hot_rows, other_rows) + SPLIT - 1) // SPLIT)
    airborne_mask = label_rows < airborne_expert
    selected_experts = jnp.sum(jnp.where(airborne_mask, label_rows, 0), axis=1)
    merge_results = jnp.sum(jnp.where(airborne_mask, probabilities, 0.0), axis=1)
    member = (
        selected_experts[:, None] == jnp.arange(airborne_expert, dtype=jnp.int32)[None, :]
    ).astype(jnp.int32)
    earlier = jnp.cumsum(member, axis=0) - member
    slot = jnp.sum(earlier * member, axis=1)
    code = selected_experts * capacity + slot
    table = (
        code[None, :] == jnp.arange(airborne_expert * capacity, dtype=jnp.int32)[:, None]
    ).astype(jnp.bfloat16)
    packed = (
        jnp.dot(table, normed, preferred_element_type=jnp.float32)
        .astype(jnp.bfloat16)
        .reshape(airborne_expert, capacity, D)
    )
    outgoing = jnp.repeat(packed, SPLIT, axis=0)
    received = lax.all_to_all(outgoing, "expert", split_axis=0, concat_axis=0, tiled=True)
    row_block = received.reshape(devices * capacity, D)
    gated = jnp.dot(row_block, gate_proj[0, 0], preferred_element_type=jnp.float32)
    lifted = jnp.dot(row_block, up_proj[0, 0], preferred_element_type=jnp.float32)
    activation = (jax.nn.silu(gated) * lifted).astype(jnp.bfloat16)
    partial_value = jnp.dot(
        activation, down_proj[0, 0], preferred_element_type=jnp.float32
    ).reshape(devices, capacity, D)
    returned = lax.all_to_all(
        partial_value.astype(jnp.bfloat16), "expert", split_axis=0, concat_axis=0, tiled=True
    ).astype(partial_value.dtype)
    summed = jnp.sum(returned.reshape(airborne_expert, SPLIT, capacity, D), axis=1).reshape(
        airborne_expert * capacity, D
    )
    routed = summed[code]
    result = (mixed + merge_results[:, None] * routed).astype(jnp.bfloat16)
    return shifted(result[None], "section", 1)


def solution(mesh):
    in_specs = (
        P("section", "expert", None),
        P("section", "expert", None),
        P("section", None, "expert", None),
        P("section", None, "expert", None),
        P("section"),
        P("section", "expert", None),
        P("section", None),
        P("section", None, None),
        P("section", "expert", None),
        P("section", "expert", None, None),
        P("section", "expert", None, None),
        P("section", "expert", None, None),
    )
    out_specs = P("section", "expert", None)
    return jax.shard_map(shards, mesh=mesh, in_specs=in_specs, out_specs=out_specs, check_vma=False)
```

profile of v0, /device:TPU:16, one launch (start us, length us, event | category | flops | bytes accessed | tf_op | source)
XLA Modules:
  0.0 526.3 jit_solution(17243223187011428407)
XLA Ops:
  8.3 13.9 %all_gather.6 = bf16[2,768,256]{2,0,1:T(2,128)(2,1)S(1)} all-gather(bf16[2,96,256]{2,0,1:T(2,128)(2,1)S(1)} %pad_maximum_fusion), channel_id=1, replica_groups=mesh['section'=4,'expert'=8] {'expert'}, dimensions={1}, use_global_device_ids=true | all-gather | bytes 884736 | tf_op jit(solution)/shard_map/all_gather | solution.py:105
  22.2 2.2 fusion.53
  24.4 2.3 copy.46
  26.7 2.0 copy.48
  28.7 3.0 copy.47
  31.8 2.4 fusion.2
  34.2 2.1 fusion.6
  36.3 2.1 divide_convert_fusion
  38.5 1.1 copy.38
  40.2 256.7 %all-gather.3.cloned.1.call-done = bf16[1,4096,4096]{2,1,0:T(8,128)(2,1)} async-done(((bf16[1,512,4096]{2,1,0:T(8,128)(2,1)}), bf16[1,4096,4096]{2,1,0:T(8,128)(2,1)}) %all-gather.3.cloned.1.call-update) | async-done | bytes 33554448 | tf_op jit(solution)/shard_map/all_gather | solution.py:116
  296.9 16.8 %multiply_reduce_fusion = (f32[64]{0:T(128)S(1)}, f32[64,4096]{1,0:T(8,128)S(1)}) fusion(bf16[1,4096,4096]{2,1,0:T(8,128)(2,1)} %all-gather.3.cloned.1.call-done, bf16[8,8,32,128]{3,2,1,0:T(8,128)(2,1)} %bitcast.109, bf16[1,64,4096]{2,1,0:T(8,128)(2,1)} %param.12), kind=kOutput, calls=%fused_computation.27 | convolution fusion | flops 2148532224 | bytes 35651840 | tf_op jit(solution)/shard_map/dot_general | solution.py:114
  314.7 84.6 %all_to_all.10 = bf16[8,56,4096]{2,1,0:T(8,128)(2,1)S(1)} all-to-all(bf16[8,56,4096]{2,1,0:T(8,128)(2,1)S(1)} %bitcast.104), channel_id=1, replica_groups=mesh['section'=4,'expert'=8] {'expert'}, dimensions={0} | all-to-all | bytes 7340032 | tf_op jit(solution)/shard_map/all_to_all | solution.py:149
  399.3 2.1 fusion.11
  401.4 2.1 fusion.25
  403.5 3.9 convolution_convert_fusion
  407.4 7.7 %all-to-all-start.1 = ((bf16[8,56,4096]{2,1,0:T(8,128)(2,1)}), bf16[8,56,4096]{2,1,0:T(8,128)(2,1)}, u32[]{:S(2)}, u32[]{:S(2)}) async-start(bf16[8,56,4096]{2,1,0:T(8,128)(2,1)} %convolution_convert_fusion), calls=%async_computation.1 | async-start | bytes 7340032 | tf_op jit(solution)/shard_map/all_to_all | solution.py:157
  415.2 1.9 fusion.28
  417.8 76.9 %all-to-all-done.1 = bf16[8,56,4096]{2,1,0:T(8,128)(2,1)} async-done(((bf16[8,56,4096]{2,1,0:T(8,128)(2,1)}), bf16[8,56,4096]{2,1,0:T(8,128)(2,1)}, u32[]{:S(2)}, u32[]{:S(2)}) %all-to-all-start.1) | async-done | bytes 3670048 | tf_op jit(solution)/shard_map/all_to_all | solution.py:157
  494.6 4.1 convert_reduce_fusion
  498.7 3.8 gather_fusion
  502.6 1.7 fusion.32
  504.3 1.5 collective-permute-start
  505.8 12.9 %collective-permute-done = bf16[1,64,4096]{2,1,0:T(8,128)(2,1)S(1)} collective-permute-done((bf16[1,64,4096]{2,1,0:T(8,128)(2,1)S(1)}, bf16[1,64,4096]{2,1,0:T(8,128)(2,1)S(1)}, u32[]{:S(2)}, u32[]{:S(2)}) %collective-permute-start) | collective-permute-done | bytes 524320 | tf_op jit(solution)/shard_map/ppermute | solution.py:18
  518.7 0.8 copy.66
  (44 shorter events, 3.3 us)
Async XLA Ops:
  6.5 396.9 %copy-start = (bf16[1,1,384,4096]{3,2,1,0:T(8,128)(2,1)S(1)}, bf16[1,1,384,4096]{3,2,1,0:T(8,128)(2,1)}, u32[]{:S(2)}) copy-start(bf16[1,1,384,4096]{3,2,1,0:T(8,128)(2,1)} %param.23) | copy-start | bytes 9437188
  6.5 1.5 copy-start.3
  6.5 1.6 copy-start.4
  6.5 290.4 %all-gather.3.cloned.1.call-start = ((), (), s32[]{:S(2)}) async-start(), calls=%async_computation.2 | async-start | bytes 37748736 | tf_op jit(solution)/shard_map/all_gather | solution.py:116
  34.2 2.1 copy-start.2
  36.3 3.3 copy-start.5
  36.3 3.3 copy-start.6
  313.7 85.6 %copy-start.1 = (f32[64,4096]{1,0:T(8,128)}, f32[64,4096]{1,0:T(8,128)S(1)}, u32[]{:S(2)}) copy-start(f32[64,4096]{1,0:T(8,128)S(1)} %get-tuple-element.14) | copy-start | bytes 3145732
  314.7 84.7 %copy-start.7 = (bf16[1,1,4096,384]{3,2,1,0:T(8,128)(2,1)S(1)}, bf16[1,1,4096,384]{3,2,1,0:T(8,128)(2,1)}, u32[]{:S(2)}) copy-start(bf16[1,1,4096,384]{3,2,1,0:T(8,128)(2,1)} %param.21) | copy-start | bytes 9437188
  399.3 2.1 copy-start.8
  407.4 87.2 %all-to-all-start.1 = ((bf16[8,56,4096]{2,1,0:T(8,128)(2,1)}), bf16[8,56,4096]{2,1,0:T(8,128)(2,1)}, u32[]{:S(2)}, u32[]{:S(2)}) async-start(bf16[8,56,4096]{2,1,0:T(8,128)(2,1)} %convolution_convert_fusion), calls=%async_computation.1 | async-start | bytes 7340032 | tf_op jit(solution)/shard_map/all_to_all | solution.py:157
  504.3 14.4 %collective-permute-start = (bf16[1,64,4096]{2,1,0:T(8,128)(2,1)S(1)}, bf16[1,64,4096]{2,1,0:T(8,128)(2,1)S(1)}, u32[]{:S(2)}, u32[]{:S(2)}) collective-permute-start(bf16[1,64,4096]{2,1,0:T(8,128)(2,1)S(1)} %fusion.32), channel_id=1, source_target_pairs={{0,8},{8,16},{16,24},{24,0},{1,9},{9,17},{17,25},{25,1},{2,10},{10... | collective-permute-start | bytes 1572872 | tf_op jit(solution)/shard_map/ppermute | solution.py:18
Sparse Core Ops, SparseCore 0:
  9.0 287.9 all-gather.2
where the time goes:
time: 531 us; the launch traced here: 526 us
  waiting for transfers between devices  347 us (65%)
  blocking collectives  98.5 us (19%)
  matrix products  31.7 us (6%)
  local copies, waits for them, and re-layouts  15.9 us (3%)
  between operations  14.4 us (3%)
  other arithmetic  9.39 us (2%)
  starting transfers between devices  9.27 us (2%)
    all_gather x1, waiting for transfers between devices, shards(): lax.all_gather(out_proj[0], 'expert', axis=0, tiled=True)  257 us
    all_to_all x1, blocking collectives, shards(): lax.all_to_all(outgoing, 'expert', split_axis=0, concat_axis=0, tiled=True)  84.6 us
    all_to_all x1, waiting for transfers between devices, shards(): lax.all_to_all(partial_value.astype(jnp.bfloat16), 'expert', split_axis=0...  76.9 us
    dot_general x1, matrix products, shards(): jnp.dot(attended, lax.all_gather(out_proj[0], 'expert', axis=0, tiled=Tru...  16.8 us
    all_gather x1, blocking collectives, shards(): every_key_value = lax.all_gather(joined_rows, 'expert', axis=1, tiled=True)  13.9 us
    ppermute x1, waiting for transfers between devices, shifted(): lax.ppermute(shard, axis, [(i, (i + by) % length) for i in range(length)])  12.9 us
  transfers between devices with their start and end apart: 3, of which 3 were waited for; matrix products, arithmetic and copies ran while one was open for 4% of the time, Pallas kernels for 0%

commit v1 on v0

--- a/solution.py
+++ b/solution.py
@@ -111,11 +111,11 @@
         .reshape(section_tokens, QUERY_HEADS * HEAD_SIZE)
         .astype(jnp.bfloat16)
     )
-    projected = jnp.dot(
-        attended,
-        lax.all_gather(out_proj[0], "expert", axis=0, tiled=True),
-        preferred_element_type=jnp.float32,
-    )
+    features = lax.all_to_all(attended, "expert", split_axis=1, concat_axis=0, tiled=True)
+    partial_projected = jnp.dot(features, out_proj[0], preferred_element_type=jnp.float32)
+    projected = lax.psum_scatter(
+        partial_projected.astype(jnp.bfloat16), "expert", scatter_dimension=0, tiled=True
+    ).astype(jnp.float32)
     mixed = hidden[0].astype(jnp.float32) + projected
     inverse = lax.rsqrt(jnp.mean(mixed * mixed, axis=1, keepdims=True) + 1e-06)
     normed = (mixed * inverse * norm_gain[0].astype(jnp.float32)[None, :]).astype(jnp.bfloat16)

time: 531 us -> 340 us (0.64)
  waiting for transfers between devices: 347 us -> 138 us
  blocking collectives: 98.5 us -> 118 us
  matrix products: 31.7 us -> 22.6 us
  local copies, waits for them, and re-layouts: 15.9 us -> 21.4 us
    all_gather x1 -> x0, waiting for transfers between devices: 257 us -> none  [shards(): lax.all_gather(out_proj[0], 'expert', axis=0, tiled=True)]
    reduce_scatter x0 -> x1, waiting for transfers between devices: none -> 48 us  [shards(): lax.psum_scatter(partial_projected.astype(jnp.bfloat16), 'expert', scatte...]
    all_to_all x0 -> x1, blocking collectives: none -> 18.9 us  [shards(): lax.all_to_all(attended, 'expert', split_axis=1, concat_axis=0, tiled=True)]
    dot_general x1, matrix products: 16.8 us -> 6.46 us  [shards(): jnp.dot(features, out_proj[0], preferred_element_type=jnp.float32)]
  transfers between devices with their start and end apart: 3 -> 3, of which waited for: 3 -> 3; matrix products, arithmetic and copies ran while one was open for 4% -> 1% of each run, Pallas kernels for 0% -> 0%
where the time goes in v1:
time: 340 us; the launch traced here: 334 us
  waiting for transfers between devices  138 us (41%)
  blocking collectives  118 us (35%)
  matrix products  22.6 us (7%)
  local copies, waits for them, and re-layouts  21.4 us (6%)
  between operations  14.4 us (4%)
  other arithmetic  10.9 us (3%)
  starting transfers between devices  9.25 us (3%)
    all_to_all x1, blocking collectives, shards(): lax.all_to_all(outgoing, 'expert', split_axis=0, concat_axis=0, tiled=True)  85.2 us
    all_to_all x1, waiting for transfers between devices, shards(): lax.all_to_all(partial_value.astype(jnp.bfloat16), 'expert', split_axis=0...  76.8 us
    reduce_scatter x1, waiting for transfers between devices, shards(): lax.psum_scatter(partial_projected.astype(jnp.bfloat16), 'expert', scatte...  48 us
    all_to_all x1, blocking collectives, shards(): lax.all_to_all(attended, 'expert', split_axis=1, concat_axis=0, tiled=True)  18.9 us
    all_gather x1, blocking collectives, shards(): every_key_value = lax.all_gather(joined_rows, 'expert', axis=1, tiled=True)  13.9 us
    ppermute x1, waiting for transfers between devices, shifted(): lax.ppermute(shard, axis, [(i, (i + by) % length) for i in range(length)])  12.9 us
    unnamed x19, local copies, waits for them, and re-layouts  10.4 us
    all_to_all x1, starting transfers between devices, shards(): lax.all_to_all(partial_value.astype(jnp.bfloat16), 'expert', split_axis=0...  7.74 us
  transfers between devices with their start and end apart: 3, of which 3 were waited for; matrix products, arithmetic and copies ran while one was open for 1% of the time, Pallas kernels for 0%

profile of v1, /device:TPU:16, one launch (start us, length us, event | category | flops | bytes accessed | tf_op | source)
XLA Modules:
  0.0 334.3 jit_solution(17135138276701244115)
XLA Ops:
  9.2 1.9 copy.51
  11.3 13.9 %all_gather.3 = bf16[2,768,256]{2,0,1:T(2,128)(2,1)S(1)} all-gather(bf16[2,96,256]{2,0,1:T(2,128)(2,1)S(1)} %pad_maximum_fusion), channel_id=1, replica_groups=mesh['section'=4,'expert'=8] {'expert'}, dimensions={1}, use_global_device_ids=true | all-gather | bytes 884736 | tf_op jit(solution)/shard_map/all_gather | solution.py:105
  25.2 2.3 fusion.47
  27.4 2.2 copy.49
  29.6 2.9 copy.50
  32.6 2.4 fusion
  35.0 2.1 fusion.1
  37.1 2.1 divide_convert_fusion
  40.4 2.1 convert_element_type.48
  43.7 18.9 %all_to_all.26 = bf16[64,8,512]{2,0,1:T(8,128)(2,1)S(1)} all-to-all(bf16[64,8,512]{2,0,1:T(8,128)(2,1)S(1)} %copy.41), channel_id=1, replica_groups=mesh['section'=4,'expert'=8] {'expert'}, dimensions={1} | all-to-all | bytes 1048576 | tf_op jit(solution)/shard_map/all_to_all | solution.py:114
  62.6 6.5 %convolution_convert_fusion = bf16[512,4096]{1,0:T(8,128)(2,1)} fusion(bf16[512,512]{1,0:T(8,128)(2,1)S(1)} %bitcast.111, bf16[1,512,4096]{2,1,0:T(8,128)(2,1)} %param.17), kind=kOutput, calls=%fused_computation.4 | convolution fusion | flops 2149580800 | bytes 8912896 | tf_op jit(solution)/shard_map/dot_general | solution.py:115
  70.4 48.0 %reduce-scatter.2.cloned.1.call-done = bf16[64,4096]{1,0:T(8,128)(2,1)} async-done(((bf16[512,4096]{1,0:T(8,128)(2,1)}), bf16[64,4096]{1,0:T(8,128)(2,1)}) %reduce-scatter.2.cloned.1.call-update) | async-done | bytes 524304 | tf_op jit(solution)/shard_map/reduce_scatter | solution.py:116
  119.9 1.7 convolution_convert_fusion.2
  122.0 85.2 %all_to_all.27 = bf16[8,56,4096]{2,1,0:T(8,128)(2,1)S(1)} all-to-all(bf16[8,56,4096]{2,1,0:T(8,128)(2,1)S(1)} %bitcast.103), channel_id=1, replica_groups=mesh['section'=4,'expert'=8] {'expert'}, dimensions={0} | all-to-all | bytes 7340032 | tf_op jit(solution)/shard_map/all_to_all | solution.py:149
  207.3 2.1 fusion.7
  209.3 2.1 fusion.21
  211.4 3.9 %convolution_convert_fusion.1 = bf16[8,56,4096]{2,1,0:T(8,128)(2,1)} fusion(bf16[8,56,384]{2,1,0:T(8,128)(2,1)S(1)} %bitcast.117, bf16[1,1,384,4096]{3,2,1,0:T(8,128)(2,1)S(1)} %copy-done), kind=kOutput, calls=%fused_computation.5 | convolution fusion | flops 1411121152 | bytes 7159808 | tf_op jit(solution)/shard_map/dot_general | solution.py:154
  215.3 7.7 %all-to-all-start.2 = ((bf16[8,56,4096]{2,1,0:T(8,128)(2,1)}), bf16[8,56,4096]{2,1,0:T(8,128)(2,1)}, u32[]{:S(2)}, u32[]{:S(2)}) async-start(bf16[8,56,4096]{2,1,0:T(8,128)(2,1)} %convolution_convert_fusion.1), calls=%async_computation.3 | async-start | bytes 7340032 | tf_op jit(solution)/shard_map/all_to_all | solution.py:157
  223.1 1.9 fusion.24
  225.8 76.8 %all-to-all-done.2 = bf16[8,56,4096]{2,1,0:T(8,128)(2,1)} async-done(((bf16[8,56,4096]{2,1,0:T(8,128)(2,1)}), bf16[8,56,4096]{2,1,0:T(8,128)(2,1)}, u32[]{:S(2)}, u32[]{:S(2)}) %all-to-all-start.2) | async-done | bytes 3670048 | tf_op jit(solution)/shard_map/all_to_all | solution.py:157
  302.6 4.1 %convert_reduce_fusion = f32[2,56,4096]{2,1,0:T(8,128)} fusion(bf16[8,56,4096]{2,1,0:T(8,128)(2,1)} %all-to-all-done.2), kind=kLoop, calls=%fused_computation.1 | loop fusion | flops 3211264 | bytes 5505024 | tf_op jit(solution)/shard_map/reduce_sum | solution.py:160
  306.7 3.8 %gather_fusion = f32[64,4096]{1,0:T(8,128)} fusion(f32[112,4096]{1,0:T(8,128)} %bitcast.102, s32[1024]{0:T(1024)S(1)} %pad_clamp_fusion), kind=kCustom, calls=%fused_computation | custom fusion | bytes 2097408 | tf_op jit(solution)/shard_map/gather | solution.py:163
  310.5 1.7 fusion.28
  313.7 12.9 %collective-permute-done = bf16[1,64,4096]{2,1,0:T(8,128)(2,1)S(1)} collective-permute-done((bf16[1,64,4096]{2,1,0:T(8,128)(2,1)S(1)}, bf16[1,64,4096]{2,1,0:T(8,128)(2,1)S(1)}, u32[]{:S(2)}, u32[]{:S(2)}) %collective-permute-start) | collective-permute-done | bytes 524320 | tf_op jit(solution)/shard_map/ppermute | solution.py:18
  (42 shorter events, 10.7 us)
Async XLA Ops:
  6.5 204.9 %copy-start = (bf16[1,1,384,4096]{3,2,1,0:T(8,128)(2,1)S(1)}, bf16[1,1,384,4096]{3,2,1,0:T(8,128)(2,1)}, u32[]{:S(2)}) copy-start(bf16[1,1,384,4096]{3,2,1,0:T(8,128)(2,1)} %param.23) | copy-start | bytes 9437188
  6.5 111.9 %reduce-scatter.2.cloned.1.call-start = ((), (), s32[]{:S(2)}) async-start(), calls=%async_computation.4 | async-start | bytes 4718592 | tf_op jit(solution)/shard_map/reduce_scatter | solution.py:116
  35.0 2.1 copy-start.1
  69.1 0.7 copy-start.2
  69.1 0.7 copy-start.3
  122.0 85.3 %copy-start.4 = (bf16[1,1,4096,384]{3,2,1,0:T(8,128)(2,1)S(1)}, bf16[1,1,4096,384]{3,2,1,0:T(8,128)(2,1)}, u32[]{:S(2)}) copy-start(bf16[1,1,4096,384]{3,2,1,0:T(8,128)(2,1)} %param.21) | copy-start | bytes 9437188
  207.3 2.1 copy-start.5
  215.3 87.2 %all-to-all-start.2 = ((bf16[8,56,4096]{2,1,0:T(8,128)(2,1)}), bf16[8,56,4096]{2,1,0:T(8,128)(2,1)}, u32[]{:S(2)}, u32[]{:S(2)}) async-start(bf16[8,56,4096]{2,1,0:T(8,128)(2,1)} %convolution_convert_fusion.1), calls=%async_computation.3 | async-start | bytes 7340032 | tf_op jit(solution)/shard_map/all_to_all | solution.py:157
  312.2 14.4 %collective-permute-start = (bf16[1,64,4096]{2,1,0:T(8,128)(2,1)S(1)}, bf16[1,64,4096]{2,1,0:T(8,128)(2,1)S(1)}, u32[]{:S(2)}, u32[]{:S(2)}) collective-permute-start(bf16[1,64,4096]{2,1,0:T(8,128)(2,1)S(1)} %fusion.28), channel_id=1, source_target_pairs={{0,8},{8,16},{16,24},{24,0},{1,9},{9,17},{17,25},{25,1},{2,10},{10... | collective-permute-start | bytes 1572872 | tf_op jit(solution)/shard_map/ppermute | solution.py:18
Sparse Core Ops, SparseCore 0:
  69.2 49.1 reduce-scatter.1

commit v2 on v1

--- a/solution.py
+++ b/solution.py
@@ -1,8 +1,11 @@
+import functools
 import math
 
 import jax
 import jax.numpy as jnp
 from jax import lax
+from jax.experimental import pallas as pl
+from jax.experimental.pallas import tpu as pltpu
 from jax.sharding import PartitionSpec as P
 
 D = 4096
@@ -165,6 +168,629 @@
     return shifted(result[None], "section", 1)
 
 
+MESH = pl.DeviceIdType.MESH
+PIECES = 4
+
+
+def tick_kernel(
+    sizes,
+    query_ref,
+    rows_ref,
+    hidden_ref,
+    fill_ref,
+    gain_ref,
+    label_ref,
+    out_proj_hbm,
+    router_hbm,
+    gate_hbm,
+    up_hbm,
+    down_hbm,
+    out_ref,
+    out_proj_ref,
+    router_ref,
+    gate_ref,
+    up_ref,
+    down_ref,
+    query_all,
+    rows_all,
+    keys_ref,
+    values_ref,
+    attended_ref,
+    pair_send,
+    pair_recv,
+    part_ref,
+    right_send,
+    right_recv,
+    left_send,
+    left_recv,
+    normed_ref,
+    mixed_ref,
+    combine_ref,
+    expert_send,
+    expert_recv,
+    routed_ref,
+    back_right_send,
+    back_right_recv,
+    back_left_send,
+    back_left_recv,
+    result_ref,
+    weight_sem,
+    query_send_sem,
+    query_recv_sem,
+    rows_send_sem,
+    rows_recv_sem,
+    share_send_sem,
+    share_recv_sem,
+    pair_sem,
+    right_sem,
+    left_sem,
+    norm_sem,
+    expert_sem,
+    back_right_sem,
+    back_left_sem,
+    out_sem,
+):
+    devices, sections, tokens, cache_rows, heads, head_group, local_experts = sizes
+    chips = devices // 2
+    width = hidden_ref.shape[1] // PIECES
+    section = lax.axis_index("section")
+    me = lax.axis_index("expert")
+    chip, core = me // 2, me % 2
+    partner = me + 1 - 2 * core
+    next_section = (section + 1) % sections
+    before_section = (section + sections - 1) % sections
+    right = (me + 2) % devices
+    left = (me + devices - 2) % devices
+
+    def remote(source, target, send_sem, recv_sem, to, to_section=None):
+        return pltpu.make_async_remote_copy(
+            src_ref=source,
+            dst_ref=target,
+            send_sem=send_sem,
+            recv_sem=recv_sem,
+            device_id=(section if to_section is None else to_section, to),
+            device_id_type=MESH,
+        )
+
+    weights = [
+        pltpu.make_async_copy(source, target, weight_sem.at[at])
+        for at, (source, target) in enumerate(
+            [
+                (out_proj_hbm, out_proj_ref),
+                (gate_hbm, gate_ref),
+                (up_hbm, up_ref),
+                (down_hbm, down_ref),
+                (router_hbm, router_ref),
+            ]
+        )
+    ]
+
+    barrier = pltpu.get_barrier_semaphore()
+    for step in range(1, devices):
+        pl.semaphore_signal(
+            barrier, inc=1, device_id=(section, (me + step) % devices), device_id_type=MESH
+        )
+    pl.semaphore_signal(barrier, inc=1, device_id=(next_section, me), device_id_type=MESH)
+    pl.semaphore_signal(barrier, inc=1, device_id=(before_section, me), device_id_type=MESH)
+    pl.semaphore_wait(barrier, devices + 1)
+
+    def key_head(chip_at):
+        return (chip_at * 2 * heads) // head_group
+
+    def query_copy(step):
+        to = (me + step) % devices
+        return remote(
+            query_ref.at[to], query_all.at[me], query_send_sem.at[step], query_recv_sem.at[step], to
+        )
+
+    def rows_copy(step):
+        to_chip = (chip + step) % chips
+        return remote(
+            rows_ref.at[key_head(to_chip)],
+            rows_all.at[me],
+            rows_send_sem.at[step],
+            rows_recv_sem.at[step],
+            2 * to_chip + core,
+        )
+
+    def share_copy(step):
+        slot = 2 * ((chip + chips - step) % chips) + core
+        return remote(
+            rows_all.at[slot],
+            rows_all.at[slot],
+            share_send_sem.at[step],
+            share_recv_sem.at[step],
+            partner,
+        )
+
+    for step in range(1, chips):
+        rows_copy(step).start()
+    for step in range(1, devices):
+        query_copy(step).start()
+    for copy in weights:
+        copy.start()
+    query_all[me] = query_ref[me]
+    rows_all[me] = rows_ref[key_head(chip)]
+    for step in range(chips):
+        if step > 0:
+            rows_copy(step).wait_recv()
+        share_copy(step).start()
+    for step in range(chips):
+        share_copy(step).wait_recv()
+
+    for device in range(devices):
+        at = 0
+        for ref in (keys_ref, values_ref):
+            start = devices * cache_rows + device * tokens
+            ref[start : start + tokens] = rows_all[device, at : at + tokens]
+            at += tokens
+        for ref in (keys_ref, values_ref):
+            start = device * cache_rows
+            ref[start : start + cache_rows] = rows_all[device, at : at + cache_rows]
+            at += cache_rows
+    for step in range(1, devices):
+        query_copy(step).wait_recv()
+    weights[0].wait()
+
+    fill = fill_ref[0]
+    total_rows = keys_ref.shape[0]
+    cached = devices * cache_rows
+    group_rows = heads * tokens
+    column = lax.broadcasted_iota(jnp.int32, (group_rows, total_rows), 1)
+    row_token = lax.broadcasted_iota(jnp.int32, (group_rows, total_rows), 0) % tokens
+
+    def home_of(step):
+        return jnp.where(step % 2 == 0, step // 2, chips - 1 - step // 2)
+
+    def pair_copy(step):
+        return remote(
+            pair_send.at[step], pair_recv.at[step], pair_sem.at[0, step], pair_sem.at[1, step], partner
+        )
+
+    def right_copy(step, piece):
+        return remote(
+            right_send.at[step, piece],
+            right_recv.at[step, piece],
+            right_sem.at[0, step, piece],
+            right_sem.at[1, step, piece],
+            right,
+        )
+
+    def left_copy(step, piece):
+        return remote(
+            left_send.at[step, piece],
+            left_recv.at[step, piece],
+            left_sem.at[0, step, piece],
+            left_sem.at[1, step, piece],
+            left,
+        )
+
+    def norm_copy(step):
+        return remote(
+            normed_ref.at[step, 0],
+            normed_ref.at[step, 1],
+            norm_sem.at[0, step],
+            norm_sem.at[1, step],
+            partner,
+        )
+
+    def expert_copy(step):
+        return remote(
+            expert_send.at[step],
+            expert_recv.at[step],
+            expert_sem.at[0, step],
+            expert_sem.at[1, step],
+            partner,
+        )
+
+    def back_right_copy(step, piece):
+        return remote(
+            back_right_send.at[step, piece],
+            back_right_recv.at[step, piece],
+            back_right_sem.at[0, step, piece],
+            back_right_sem.at[1, step, piece],
+            right,
+        )
+
+    def back_left_copy(step, piece):
+        return remote(
+            back_left_send.at[step, piece],
+            back_left_recv.at[step, piece],
+            back_left_sem.at[0, step, piece],
+            back_left_sem.at[1, step, piece],
+            left,
+        )
+
+    def out_copy(piece):
+        return remote(
+            result_ref.at[piece],
+            out_ref.at[:, pl.ds(piece * width, width)],
+            out_sem.at[0, piece],
+            out_sem.at[1, piece],
+            me,
+            next_section,
+        )
+
+    def project(step, carry):
+        home = home_of(step)
+        for which in range(2):
+            owner = 2 * home + (core if which == 0 else 1 - core)
+            scores = (
+                lax.dot_general(
+                    query_all[owner],
+                    keys_ref[...],
+                    (((1,), (1,)), ((), ())),
+                    preferred_element_type=jnp.float32,
+                )
+                * (1.0 / math.sqrt(HEAD_SIZE))
+            )
+            limit = jnp.where(column < cached, fill, cached + owner * tokens + row_token + 1)
+            visible = column < limit
+            masked = jnp.where(visible, scores, -1e30)
+            highest = jnp.max(masked, axis=1, keepdims=True)
+            weight = jnp.where(visible, jnp.exp(masked - highest), 0.0)
+            totals = jnp.sum(weight, axis=1, keepdims=True)
+            mean = (
+                jnp.dot(
+                    weight.astype(jnp.bfloat16), values_ref[...], preferred_element_type=jnp.float32
+                )
+                / totals
+            ).astype(jnp.bfloat16)
+            for head in range(heads):
+                attended_ref[
+                    which * tokens : (which + 1) * tokens, head * HEAD_SIZE : (head + 1) * HEAD_SIZE
+                ] = mean[head * tokens : (head + 1) * tokens]
+        for piece in range(PIECES):
+            product = jnp.dot(
+                attended_ref[...],
+                out_proj_ref[:, piece * width : (piece + 1) * width],
+                preferred_element_type=jnp.float32,
+            )
+            part_ref[step, piece] = product[:tokens]
+            pair_send[step, piece] = product[tokens:].astype(jnp.bfloat16)
+        pair_copy(step).start()
+
+        @pl.when(home == chip)
+        def _():
+            for piece in range(PIECES):
+                part_ref[step, piece] += hidden_ref[
+                    :, piece * width : (piece + 1) * width
+                ].astype(jnp.float32)
+
+        pair_copy(step).wait_recv()
+        for piece in range(PIECES):
+            part_ref[step, piece] += pair_recv[step, piece].astype(jnp.float32)
+
+            @pl.when(chip == 0)
+            def _():
+                right_send[step, piece] = part_ref[step, piece].astype(jnp.bfloat16)
+                right_copy(step, piece).start()
+
+            @pl.when(chip == chips - 1)
+            def _():
+                left_send[step, piece] = part_ref[step, piece].astype(jnp.bfloat16)
+                left_copy(step, piece).start()
+
+        return carry
+
+    lax.fori_loop(0, chips, project, 0)
+    for copy in weights[1:]:
+        copy.wait()
+    my_expert = (me // SPLIT).astype(jnp.float32)
+    select_at = 2 * tokens + 2 * cache_rows
+
+    def layer(step, carry):
+        home = home_of(step)
+        for piece in range(PIECES):
+
+            @pl.when(chip > 0)
+            def _():
+                right_copy(step, piece).wait_recv()
+
+                @pl.when(chip < chips - 1)
+                def _():
+                    right_send[step, piece] = (
+                        part_ref[step, piece] + right_recv[step, piece].astype(jnp.float32)
+                    ).astype(jnp.bfloat16)
+                    right_copy(step, piece).start()
+
+            @pl.when(chip < chips - 1)
+            def _():
+                left_copy(step, piece).wait_recv()
+
+                @pl.when(chip > 0)
+                def _():
+                    left_send[step, piece] = (
+                        part_ref[step, piece] + left_recv[step, piece].astype(jnp.float32)
+                    ).astype(jnp.bfloat16)
+                    left_copy(step, piece).start()
+
+            @pl.when(chip > 0)
+            def _():
+                part_ref[step, piece] += right_recv[step, piece].astype(jnp.float32)
+
+            @pl.when(chip < chips - 1)
+            def _():
+                part_ref[step, piece] += left_recv[step, piece].astype(jnp.float32)
+
+        squares = jnp.zeros((tokens, 1), jnp.float32)
+        for piece in range(PIECES):
+            mixed = part_ref[step, piece]
+            squares += jnp.sum(mixed * mixed, axis=1, keepdims=True)
+        inverse = lax.rsqrt(squares / (PIECES * width) + 1e-06)
+        for piece in range(PIECES):
+            columns = slice(piece * width, (piece + 1) * width)
+            normed_ref[step, 0, :, columns] = (
+                part_ref[step, piece] * inverse * gain_ref[:, columns].astype(jnp.float32)
+            ).astype(jnp.bfloat16)
+        norm_copy(step).start()
+
+        @pl.when(home == chip)
+        def _():
+            for piece in range(PIECES):
+                mixed_ref[piece] = part_ref[step, piece]
+            logits = jnp.dot(
+                normed_ref[step, 0], router_ref[...], preferred_element_type=jnp.float32
+            )
+            labels = label_ref[...]
+            expert_at = lax.broadcasted_iota(jnp.int32, logits.shape, 1)
+            picked = []
+            for at in range(labels.shape[1]):
+                match = labels[:, at : at + 1] == expert_at
+                picked.append(jnp.sum(jnp.where(match, logits, 0.0), axis=1, keepdims=True))
+            highest = picked[0]
+            for value in picked[1:]:
+                highest = jnp.maximum(highest, value)
+            total = jnp.zeros_like(highest)
+            chosen = jnp.zeros_like(highest)
+            for at, value in enumerate(picked):
+                weight = jnp.exp(value - highest)
+                total += weight
+                chosen += jnp.where(labels[:, at : at + 1] < local_experts, weight, 0.0)
+            combine_ref[...] = jnp.broadcast_to(chosen / total, combine_ref.shape)
+
+        norm_copy(step).wait_recv()
+        rows = normed_ref[step].reshape(2 * tokens, PIECES * width)
+        gated = jnp.dot(rows, gate_ref[...], preferred_element_type=jnp.float32)
+        lifted = jnp.dot(rows, up_ref[...], preferred_element_type=jnp.float32)
+        activation = gated / (1.0 + jnp.exp(-gated)) * lifted
+        selected = jnp.concatenate(
+            [
+                rows_all[2 * home + core, select_at : select_at + tokens],
+                rows_all[2 * home + 1 - core, select_at : select_at + tokens],
+            ],
+            axis=0,
+        ).astype(jnp.float32)[:, :1]
+        activation = jnp.where(selected == my_expert, activation, 0.0).astype(jnp.bfloat16)
+        for piece in range(PIECES):
+            product = jnp.dot(
+                activation,
+                down_ref[:, piece * width : (piece + 1) * width],
+                preferred_element_type=jnp.float32,
+            )
+            routed_ref[step, piece] = product[:tokens]
+            expert_send[step, piece] = product[tokens:].astype(jnp.bfloat16)
+        expert_copy(step).start()
+        expert_copy(step).wait_recv()
+        for piece in range(PIECES):
+            routed_ref[step, piece] += expert_recv[step, piece].astype(jnp.float32)
+
+            @pl.when((chip == 0) & (home > 0))
+            def _():
+                back_right_send[step, piece] = routed_ref[step, piece].astype(jnp.bfloat16)
+                back_right_copy(step, piece).start()
+
+            @pl.when((chip == chips - 1) & (home < chips - 1))
+            def _():
+                back_left_send[step, piece] = routed_ref[step, piece].astype(jnp.bfloat16)
+                back_left_copy(step, piece).start()
+
+        return carry
+
+    lax.fori_loop(0, chips, layer, 0)
+
+    def back(step, carry):
+        home = home_of(step)
+        for piece in range(PIECES):
+
+            @pl.when((chip > 0) & (chip <= home))
+            def _():
+                back_right_copy(step, piece).wait_recv()
+                routed_ref[step, piece] += back_right_recv[step, piece].astype(jnp.float32)
+
+            @pl.when((chip > 0) & (chip < home))
+            def _():
+                back_right_send[step, piece] = routed_ref[step, piece].astype(jnp.bfloat16)
+                back_right_copy(step, piece).start()
+
+            @pl.when((chip < chips - 1) & (chip >= home))
+            def _():
+                back_left_copy(step, piece).wait_recv()
+                routed_ref[step, piece] += back_left_recv[step, piece].astype(jnp.float32)
+
+            @pl.when((chip < chips - 1) & (chip > home))
+            def _():
+                back_left_send[step, piece] = routed_ref[step, piece].astype(jnp.bfloat16)
+                back_left_copy(step, piece).start()
+
+            @pl.when(chip == home)
+            def _():
+                result_ref[piece] = (
+                    mixed_ref[piece] + combine_ref[:, :1] * routed_ref[step, piece]
+                ).astype(jnp.bfloat16)
+                out_copy(piece).start()
+
+        return carry
+
+    lax.fori_loop(0, chips, back, 0)
+
+    def drain(step, carry):
+        home = home_of(step)
+        pair_copy(step).wait_send()
+        norm_copy(step).wait_send()
+        expert_copy(step).wait_send()
+        for piece in range(PIECES):
+
+            @pl.when(chip < chips - 1)
+            def _():
+                right_copy(step, piece).wait_send()
+
+            @pl.when(chip > 0)
+            def _():
+                left_copy(step, piece).wait_send()
+
+            @pl.when(chip < home)
+            def _():
+                back_right_copy(step, piece).wait_send()
+
+            @pl.when(chip > home)
+            def _():
+                back_left_copy(step, piece).wait_send()
+
+        return carry
+
+    lax.fori_loop(0, chips, drain, 0)
+    for step in range(1, chips):
+        rows_copy(step).wait_send()
+    for step in range(chips):
+        share_copy(step).wait_send()
+    for step in range(1, devices):
+        query_copy(step).wait_send()
+    for piece in range(PIECES):
+        out_copy(piece).wait()
+
+
+def fused_shards(
+    sections,
+    hidden,
+    queries,
+    fresh_kv,
+    cache_kv,
+    cache_fill,
+    out_proj,
+    norm_gain,
+    router_weight,
+    expert_labels,
+    gate_proj,
+    up_proj,
+    down_proj,
+):
+    devices = lax.axis_size("expert")
+    chips = devices // 2
+    tokens, model = hidden.shape[1:]
+    cache_rows = cache_kv.shape[2]
+    heads = QUERY_HEADS // devices
+    head_group = QUERY_HEADS // KEY_VALUE_HEADS
+    local_experts = devices // SPLIT
+    features = heads * HEAD_SIZE
+    hidden_units = gate_proj.shape[3]
+    width = model // PIECES
+    query_rows = jnp.transpose(
+        queries[0].reshape(tokens, devices, heads, HEAD_SIZE), (1, 2, 0, 3)
+    ).reshape(devices, heads * tokens, HEAD_SIZE)
+    labels = expert_labels[0]
+    selected = jnp.sum(jnp.where(labels < local_experts, labels, 0), axis=1)
+
+    def by_head(array, length):
+        return jnp.transpose(
+            array.reshape(2, length, KEY_VALUE_HEADS, HEAD_SIZE), (2, 0, 1, 3)
+        ).reshape(KEY_VALUE_HEADS, 2 * length, HEAD_SIZE)
+
+    key_rows = jnp.concatenate(
+        [
+            by_head(fresh_kv[0], tokens),
+            by_head(cache_kv[0], cache_rows),
+            jnp.broadcast_to(
+                selected.astype(jnp.bfloat16)[None, :, None], (KEY_VALUE_HEADS, tokens, HEAD_SIZE)
+            ),
+        ],
+        axis=1,
+    )
+    message = key_rows.shape[1]
+    bf16, f32 = jnp.bfloat16, jnp.float32
+    vmem = pl.BlockSpec(memory_space=pltpu.VMEM)
+    anywhere = pl.BlockSpec(memory_space=pl.ANY)
+    block = (chips, PIECES, tokens, width)
+    dma = pltpu.SemaphoreType.DMA
+    sizes = (devices, sections, tokens, cache_rows, heads, head_group, local_experts)
+    total_rows = devices * (tokens + cache_rows)
+    result = pl.pallas_call(
+        functools.partial(tick_kernel, sizes),
+        out_shape=jax.ShapeDtypeStruct((tokens, model), bf16),
+        in_specs=[vmem, vmem, vmem, pl.BlockSpec(memory_space=pltpu.SMEM), vmem, vmem]
+        + [anywhere] * 5,
+        out_specs=vmem,
+        scratch_shapes=[
+            pltpu.VMEM((features, model), bf16),
+            pltpu.VMEM(router_weight.shape[1:], bf16),
+            pltpu.VMEM((model, hidden_units), bf16),
+            pltpu.VMEM((model, hidden_units), bf16),
+            pltpu.VMEM((hidden_units, model), bf16),
+            pltpu.VMEM((devices, heads * tokens, HEAD_SIZE), bf16),
+            pltpu.VMEM((devices, message, HEAD_SIZE), bf16),
+            pltpu.VMEM((total_rows, HEAD_SIZE), bf16),
+            pltpu.VMEM((total_rows, HEAD_SIZE), bf16),
+            pltpu.VMEM((2 * tokens, features), bf16),
+            pltpu.VMEM(block, bf16),
+            pltpu.VMEM(block, bf16),
+            pltpu.VMEM(block, f32),
+            pltpu.VMEM(block, bf16),
+            pltpu.VMEM(block, bf16),
+            pltpu.VMEM(block, bf16),
+            pltpu.VMEM(block, bf16),
+            pltpu.VMEM((chips, 2, tokens, model), bf16),
+            pltpu.VMEM((PIECES, tokens, width), f32),
+            pltpu.VMEM((tokens, 128), f32),
+            pltpu.VMEM(block, bf16),
+            pltpu.VMEM(block, bf16),
+            pltpu.VMEM(block, f32),
+            pltpu.VMEM(block, bf16),
+            pltpu.VMEM(block, bf16),
+            pltpu.VMEM(block, bf16),
+            pltpu.VMEM(block, bf16),
+            pltpu.VMEM((PIECES, tokens, width), bf16),
+            dma((5,)),
+            dma((devices,)),
+            dma((devices,)),
+            dma((chips,)),
+            dma((chips,)),
+            dma((chips,)),
+            dma((chips,)),
+            dma((2, chips)),
+            dma((2, chips, PIECES)),
+            dma((2, chips, PIECES)),
+            dma((2, chips)),
+            dma((2, chips)),
+            dma((2, chips, PIECES)),
+            dma((2, chips, PIECES)),
+            dma((2, PIECES)),
+        ],
+        compiler_params=pltpu.CompilerParams(
+            collective_id=0, has_side_effects=True, vmem_limit_bytes=60 * 2**20
+        ),
+    )(
+        query_rows,
+        key_rows,
+        hidden[0],
+        cache_fill,
+        norm_gain,
+        labels,
+        out_proj[0],
+        router_weight[0],
+        gate_proj[0, 0],
+        up_proj[0, 0],
+        down_proj[0, 0],
+    )
+    return result[None]
+
+
+def fits_one_kernel(mesh):
+    devices = mesh.shape["expert"]
+    if devices % 2 or QUERY_HEADS % devices:
+        return False
+    return (QUERY_HEADS // KEY_VALUE_HEADS) % (2 * (QUERY_HEADS // devices)) == 0
+
+
 def solution(mesh):
     in_specs = (
         P("section", "expert", None),
@@ -181,4 +807,7 @@
         P("section", "expert", None, None),
     )
     out_specs = P("section", "expert", None)
-    return jax.shard_map(shards, mesh=mesh, in_specs=in_specs, out_specs=out_specs, check_vma=False)
+    body = shards
+    if fits_one_kernel(mesh):
+        body = functools.partial(fused_shards, mesh.shape["section"])
+    return jax.shard_map(body, mesh=mesh, in_specs=in_specs, out_specs=out_specs, check_vma=False)

time: 340 us -> 252 us (0.74); the launches traced: 334 us -> 252 us
  Pallas kernels: 0 us -> 244 us
  waiting for transfers between devices: 138 us -> 0 us
  blocking collectives: 118 us -> 0 us
  matrix products: 22.6 us -> 0 us
  local copies, waits for them, and re-layouts: 21.4 us -> 6.79 us
  between operations: 14.4 us -> 0.69 us
  other arithmetic: 10.9 us -> 0.86 us
  starting transfers between devices: 9.25 us -> 0 us
    pallas_call x0 -> x1, Pallas kernels: none -> 244 us  [fused_shards(): pl.pallas_call(functools.partial(tick_kernel, sizes), out_shape=jax.Shape...]
    all_to_all x2 -> x0, blocking collectives: 104 us -> none  [the longest x1 85.2 us: shards(): lax.all_to_all(outgoing, 'expert', split_axis=0, concat_axis=0, tiled=True)]
    all_to_all x1 -> x0, waiting for transfers between devices: 76.8 us -> none  [shards(): lax.all_to_all(partial_value.astype(jnp.bfloat16), 'expert', split_axis=0...]
    reduce_scatter x1 -> x0, waiting for transfers between devices: 48 us -> none  [shards(): lax.psum_scatter(partial_projected.astype(jnp.bfloat16), 'expert', scatte...]
    dot_general x8 -> x0, matrix products: 22.6 us -> none  [the longest x1 6.46 us: shards(): jnp.dot(features, out_proj[0], preferred_element_type=jnp.float32)]
    all_gather x1 -> x0, blocking collectives: 13.9 us -> none  [shards(): every_key_value = lax.all_gather(joined_rows, 'expert', axis=1, tiled=True)]
    ppermute x1 -> x0, waiting for transfers between devices: 12.9 us -> none  [shifted(): lax.ppermute(shard, axis, [(i, (i + by) % length) for i in range(length)])]
    reduce_sum x8 -> x1, other arithmetic: 8.55 us -> 0.1 us  [fused_shards(): selected = jnp.sum(jnp.where(labels < local_experts, labels, 0), axis=1)]
  transfers between devices with their start and end apart: 3 -> 0, of which waited for: 3 -> 0; matrix products, arithmetic and copies ran while one was open for 1% -> 0% of each run, Pallas kernels for 0% -> 0%
where the time goes in v2:
time: 252 us
  Pallas kernels  244 us (97%)
  local copies, waits for them, and re-layouts  6.79 us (3%)
    pallas_call x1, Pallas kernels, fused_shards(): pl.pallas_call(functools.partial(tick_kernel, sizes), out_shape=jax.Shape...  244 us

profile of v2, /device:TPU:16, one launch (start us, length us, event | category | flops | bytes accessed | tf_op | source)
XLA Modules:
  0.0 252.0 jit_solution(8302203490145818552)
XLA Ops:
  0.7 0.8 copy.16
  1.4 0.0 copy-start
  1.4 0.1 fusion
  1.5 0.1 pad.2.clone
  1.6 0.8 reshape_squeeze.11
  2.4 0.9 reshape_squeeze.10
  3.3 0.8 maximum_maximum_fusion.rows_ref
  4.1 1.4 reshape_squeeze.9
  5.5 1.0 copy.13
  6.5 0.0 copy-done
  6.5 243.6 %shard_map.118 = bf16[64,4096]{1,0:T(8,128)(2,1)} custom-call(bf16[8,256,128]{2,1,0:T(8,128)(2,1)} %bitcast.26, bf16[2,256,128]{2,1,0:T(8,128)(2,1)} %maximum_maximum_fusion.rows_ref, bf16[64,4096]{1,0:T(8,128)(2,1)} %bitcast.29, s32[1]{0:T(128)S(6)} %copy.18.fill_ref, bf16[1,4096]{1,0:T(2,128)(2,1)} %gain_ref.1, s32[64,8]{1,0:T(8,128)} %bitcast.30, ...), custom_call_target="tpu_custom_call" | custom-call | tf_op jit(solution)/shard_map/pallas_call | solution.py:717
  250.1 1.9 copy.19
  (3 shorter events, 0.0 us)
Async XLA Ops:
  1.4 5.0 %copy-start = (s32[1,64,8]{2,1,0:T(8,128)}, s32[1,64,8]{2,1,0:T(8,128)S(1)}, u32[]{:S(2)}) copy-start(s32[1,64,8]{2,1,0:T(8,128)S(1)} %copy.16) | copy-start | bytes 6148

commit v3 on v2

--- a/solution.py
+++ b/solution.py
@@ -170,16 +170,17 @@
 
 MESH = pl.DeviceIdType.MESH
 PIECES = 4
+LINE = 4
 
 
 def tick_kernel(
     sizes,
-    query_ref,
     rows_ref,
-    hidden_ref,
     fill_ref,
     gain_ref,
     label_ref,
+    query_hbm,
+    hidden_hbm,
     out_proj_hbm,
     router_hbm,
     gate_hbm,
@@ -191,6 +192,7 @@
     gate_ref,
     up_ref,
     down_ref,
+    hidden_ref,
     query_all,
     rows_all,
     keys_ref,
@@ -199,20 +201,19 @@
     pair_send,
     pair_recv,
     part_ref,
-    right_send,
-    right_recv,
-    left_send,
-    left_recv,
+    inward_send,
+    outward_send,
+    near_recv,
+    far_recv,
     normed_ref,
     mixed_ref,
     combine_ref,
     expert_send,
     expert_recv,
     routed_ref,
-    back_right_send,
-    back_right_recv,
-    back_left_send,
-    back_left_recv,
+    back_send,
+    back_recv,
+    home_recv,
     result_ref,
     weight_sem,
     query_send_sem,
@@ -222,12 +223,14 @@
     share_send_sem,
     share_recv_sem,
     pair_sem,
-    right_sem,
-    left_sem,
+    near_sem,
+    far_sem,
+    fall_sem,
     norm_sem,
     expert_sem,
-    back_right_sem,
-    back_left_sem,
+    back_sem,
+    home_send_sem,
+    home_recv_sem,
     out_sem,
 ):
     devices, sections, tokens, cache_rows, heads, head_group, local_experts = sizes
@@ -239,8 +242,12 @@
     partner = me + 1 - 2 * core
     next_section = (section + 1) % sections
     before_section = (section + sections - 1) % sections
-    right = (me + 2) % devices
-    left = (me + devices - 2) % devices
+    toward = jnp.where(chip < 2, 2, -2)
+    inward = me + toward
+    outward = (me + devices - toward) % devices
+    inner = (chip == 1) | (chip == 2)
+    side = chip // 2
+    features = query_all.shape[2]
 
     def remote(source, target, send_sem, recv_sem, to, to_section=None):
         return pltpu.make_async_remote_copy(
@@ -256,11 +263,12 @@
         pltpu.make_async_copy(source, target, weight_sem.at[at])
         for at, (source, target) in enumerate(
             [
-                (out_proj_hbm, out_proj_ref),
-                (gate_hbm, gate_ref),
-                (up_hbm, up_ref),
-                (down_hbm, down_ref),
-                (router_hbm, router_ref),
+                (out_proj_hbm.at[0], out_proj_ref),
+                (hidden_hbm.at[0], hidden_ref),
+                (gate_hbm.at[0, 0], gate_ref),
+                (up_hbm.at[0, 0], up_ref),
+                (down_hbm.at[0, 0], down_ref),
+                (router_hbm.at[0], router_ref),
             ]
         )
     ]
@@ -277,11 +285,20 @@
     def key_head(chip_at):
         return (chip_at * 2 * heads) // head_group
 
+    def query_part(to):
+        return query_hbm.at[0, :, pl.ds(pl.multiple_of(to * features, HEAD_SIZE), features)]
+
     def query_copy(step):
         to = (me + step) % devices
         return remote(
-            query_ref.at[to], query_all.at[me], query_send_sem.at[step], query_recv_sem.at[step], to
-        )
+            query_part(to),
+            query_all.at[me],
+            query_send_sem.at[step],
+            query_recv_sem.at[step],
+            to,
+        )
+
+    own_query = pltpu.make_async_copy(query_part(me), query_all.at[me], query_recv_sem.at[0])
 
     def rows_copy(step):
         to_chip = (chip + step) % chips
@@ -309,7 +326,7 @@
         query_copy(step).start()
     for copy in weights:
         copy.start()
-    query_all[me] = query_ref[me]
+    own_query.start()
     rows_all[me] = rows_ref[key_head(chip)]
     for step in range(chips):
         if step > 0:
@@ -328,9 +345,11 @@
             start = device * cache_rows
             ref[start : start + cache_rows] = rows_all[device, at : at + cache_rows]
             at += cache_rows
+    own_query.wait()
     for step in range(1, devices):
         query_copy(step).wait_recv()
-    weights[0].wait()
+    for copy in weights[:2]:
+        copy.wait()
 
     fill = fill_ref[0]
     total_rows = keys_ref.shape[0]
@@ -342,27 +361,46 @@
     def home_of(step):
         return jnp.where(step % 2 == 0, step // 2, chips - 1 - step // 2)
 
-    def pair_copy(step):
+    def piece_copy(source, target, sems, step, piece, to):
         return remote(
-            pair_send.at[step], pair_recv.at[step], pair_sem.at[0, step], pair_sem.at[1, step], partner
-        )
-
-    def right_copy(step, piece):
+            source.at[step, piece],
+            target.at[step, piece],
+            sems.at[0, step, piece],
+            sems.at[1, step, piece],
+            to,
+        )
+
+    def pair_copy(step, piece):
+        return piece_copy(pair_send, pair_recv, pair_sem, step, piece, partner)
+
+    def near_copy(step, piece):
+        return piece_copy(inward_send, near_recv, near_sem, step, piece, inward)
+
+    def far_copy(step, piece):
+        return piece_copy(inward_send, far_recv, far_sem, step, piece, inward)
+
+    def fall_copy(step, piece):
         return remote(
-            right_send.at[step, piece],
-            right_recv.at[step, piece],
-            right_sem.at[0, step, piece],
-            right_sem.at[1, step, piece],
-            right,
-        )
-
-    def left_copy(step, piece):
+            outward_send.at[step, piece],
+            far_recv.at[step, piece],
+            fall_sem.at[step, piece],
+            far_sem.at[1, step, piece],
+            outward,
+        )
+
+    def expert_copy(step, piece):
+        return piece_copy(expert_send, expert_recv, expert_sem, step, piece, partner)
+
+    def back_copy(step, piece):
+        return piece_copy(back_send, back_recv, back_sem, step, piece, inward)
+
+    def home_copy(step, piece, from_side):
         return remote(
-            left_send.at[step, piece],
-            left_recv.at[step, piece],
-            left_sem.at[0, step, piece],
-            left_sem.at[1, step, piece],
-            left,
+            back_send.at[step, piece],
+            home_recv.at[from_side, piece],
+            home_send_sem.at[step, piece],
+            home_recv_sem.at[from_side, piece],
+            2 * home_of(step) + core,
         )
 
     def norm_copy(step):
@@ -372,33 +410,6 @@
             norm_sem.at[0, step],
             norm_sem.at[1, step],
             partner,
-        )
-
-    def expert_copy(step):
-        return remote(
-            expert_send.at[step],
-            expert_recv.at[step],
-            expert_sem.at[0, step],
-            expert_sem.at[1, step],
-            partner,
-        )
-
-    def back_right_copy(step, piece):
-        return remote(
-            back_right_send.at[step, piece],
-            back_right_recv.at[step, piece],
-            back_right_sem.at[0, step, piece],
-            back_right_sem.at[1, step, piece],
-            right,
-        )
-
-    def back_left_copy(step, piece):
-        return remote(
-            back_left_send.at[step, piece],
-            back_left_recv.at[step, piece],
-            back_left_sem.at[0, step, piece],
-            back_left_sem.at[1, step, piece],
-            left,
         )
 
     def out_copy(piece):
@@ -411,13 +422,19 @@
             next_section,
         )
 
-    def project(step, carry):
+    def project(step):
         home = home_of(step)
         for which in range(2):
             owner = 2 * home + (core if which == 0 else 1 - core)
             scores = (
                 lax.dot_general(
-                    query_all[owner],
+                    jnp.concatenate(
+                        [
+                            query_all[owner, :, head * HEAD_SIZE : (head + 1) * HEAD_SIZE]
+                            for head in range(heads)
+                        ],
+                        axis=0,
+                    ),
                     keys_ref[...],
                     (((1,), (1,)), ((), ())),
                     preferred_element_type=jnp.float32,
@@ -448,7 +465,7 @@
             )
             part_ref[step, piece] = product[:tokens]
             pair_send[step, piece] = product[tokens:].astype(jnp.bfloat16)
-        pair_copy(step).start()
+            pair_copy(step, piece).start()
 
         @pl.when(home == chip)
         def _():
@@ -457,61 +474,43 @@
                     :, piece * width : (piece + 1) * width
                 ].astype(jnp.float32)
 
-        pair_copy(step).wait_recv()
-        for piece in range(PIECES):
+        for piece in range(PIECES):
+            pair_copy(step, piece).wait_recv()
             part_ref[step, piece] += pair_recv[step, piece].astype(jnp.float32)
 
-            @pl.when(chip == 0)
+            @pl.when(jnp.logical_not(inner))
             def _():
-                right_send[step, piece] = part_ref[step, piece].astype(jnp.bfloat16)
-                right_copy(step, piece).start()
-
-            @pl.when(chip == chips - 1)
-            def _():
-                left_send[step, piece] = part_ref[step, piece].astype(jnp.bfloat16)
-                left_copy(step, piece).start()
-
-        return carry
-
-    lax.fori_loop(0, chips, project, 0)
-    for copy in weights[1:]:
-        copy.wait()
+                inward_send[step, piece] = part_ref[step, piece].astype(jnp.bfloat16)
+                near_copy(step, piece).start()
+
+    def forward(step):
+        for piece in range(PIECES):
+            near_copy(step, piece).wait_recv()
+            inward_send[step, piece] = (
+                part_ref[step, piece] + near_recv[step, piece].astype(jnp.float32)
+            ).astype(jnp.bfloat16)
+            far_copy(step, piece).start()
+
     my_expert = (me // SPLIT).astype(jnp.float32)
     select_at = 2 * tokens + 2 * cache_rows
 
-    def layer(step, carry):
+    def layer(step):
         home = home_of(step)
-        for piece in range(PIECES):
-
-            @pl.when(chip > 0)
+
+        @pl.when(step == 0)
+        def _():
+            for copy in weights[2:]:
+                copy.wait()
+
+        for piece in range(PIECES):
+            far_copy(step, piece).wait_recv()
+            part_ref[step, piece] += far_recv[step, piece].astype(jnp.float32)
+
+            @pl.when(inner)
             def _():
-                right_copy(step, piece).wait_recv()
-
-                @pl.when(chip < chips - 1)
-                def _():
-                    right_send[step, piece] = (
-                        part_ref[step, piece] + right_recv[step, piece].astype(jnp.float32)
-                    ).astype(jnp.bfloat16)
-                    right_copy(step, piece).start()
-
-            @pl.when(chip < chips - 1)
-            def _():
-                left_copy(step, piece).wait_recv()
-
-                @pl.when(chip > 0)
-                def _():
-                    left_send[step, piece] = (
-                        part_ref[step, piece] + left_recv[step, piece].astype(jnp.float32)
-                    ).astype(jnp.bfloat16)
-                    left_copy(step, piece).start()
-
-            @pl.when(chip > 0)
-            def _():
-                part_ref[step, piece] += right_recv[step, piece].astype(jnp.float32)
-
-            @pl.when(chip < chips - 1)
-            def _():
-                part_ref[step, piece] += left_recv[step, piece].astype(jnp.float32)
+                outward_send[step, piece] = part_ref[step, piece].astype(jnp.bfloat16)
+                fall_copy(step, piece).start()
+                part_ref[step, piece] += near_recv[step, piece].astype(jnp.float32)
 
         squares = jnp.zeros((tokens, 1), jnp.float32)
         for piece in range(PIECES):
@@ -570,82 +569,85 @@
             )
             routed_ref[step, piece] = product[:tokens]
             expert_send[step, piece] = product[tokens:].astype(jnp.bfloat16)
-        expert_copy(step).start()
-        expert_copy(step).wait_recv()
-        for piece in range(PIECES):
+            expert_copy(step, piece).start()
+        for piece in range(PIECES):
+            expert_copy(step, piece).wait_recv()
             routed_ref[step, piece] += expert_recv[step, piece].astype(jnp.float32)
 
-            @pl.when((chip == 0) & (home > 0))
+            @pl.when(jnp.logical_not(inner) & (home != chip))
             def _():
-                back_right_send[step, piece] = routed_ref[step, piece].astype(jnp.bfloat16)
-                back_right_copy(step, piece).start()
-
-            @pl.when((chip == chips - 1) & (home < chips - 1))
+                back_send[step, piece] = routed_ref[step, piece].astype(jnp.bfloat16)
+                back_copy(step, piece).start()
+
+    def outer_chip():
+        return 3 * side
+
+    def fold(step):
+        home = home_of(step)
+        for piece in range(PIECES):
+
+            @pl.when(home != outer_chip())
             def _():
-                back_left_send[step, piece] = routed_ref[step, piece].astype(jnp.bfloat16)
-                back_left_copy(step, piece).start()
-
+                back_copy(step, piece).wait_recv()
+                routed_ref[step, piece] += back_recv[step, piece].astype(jnp.float32)
+
+            @pl.when(home != chip)
+            def _():
+                back_send[step, piece] = routed_ref[step, piece].astype(jnp.bfloat16)
+                home_copy(step, piece, side).start()
+
+    def finish(step):
+        for piece in range(PIECES):
+            for from_side in range(2):
+
+                @pl.when(chip != from_side + 1)
+                def _():
+                    home_copy(step, piece, from_side).wait_recv()
+                    routed_ref[step, piece] += home_recv[from_side, piece].astype(jnp.float32)
+
+            result_ref[piece] = (
+                mixed_ref[piece] + combine_ref[:, :1] * routed_ref[step, piece]
+            ).astype(jnp.bfloat16)
+            out_copy(piece).start()
+
+    def within(step):
+        return (step >= 0) & (step < chips)
+
+    def turn(time, carry):
+        pl.when(within(time))(lambda: project(time))
+        pl.when(within(time - 1) & inner)(lambda: forward(time - 1))
+        pl.when(within(time - 4) & inner)(lambda: fold(time - 4))
+        layer_step = time - jnp.where(inner, 2, 3)
+        pl.when(within(layer_step))(lambda: layer(layer_step))
+        ending = time - 5
+        pl.when(within(ending) & (home_of(ending) == chip))(lambda: finish(ending))
         return carry
 
-    lax.fori_loop(0, chips, layer, 0)
-
-    def back(step, carry):
-        home = home_of(step)
-        for piece in range(PIECES):
-
-            @pl.when((chip > 0) & (chip <= home))
-            def _():
-                back_right_copy(step, piece).wait_recv()
-                routed_ref[step, piece] += back_right_recv[step, piece].astype(jnp.float32)
-
-            @pl.when((chip > 0) & (chip < home))
-            def _():
-                back_right_send[step, piece] = routed_ref[step, piece].astype(jnp.bfloat16)
-                back_right_copy(step, piece).start()
-
-            @pl.when((chip < chips - 1) & (chip >= home))
-            def _():
-                back_left_copy(step, piece).wait_recv()
-                routed_ref[step, piece] += back_left_recv[step, piece].astype(jnp.float32)
-
-            @pl.when((chip < chips - 1) & (chip > home))
-            def _():
-                back_left_send[step, piece] = routed_ref[step, piece].astype(jnp.bfloat16)
-                back_left_copy(step, piece).start()
-
-            @pl.when(chip == home)
-            def _():
-                result_ref[piece] = (
-                    mixed_ref[piece] + combine_ref[:, :1] * routed_ref[step, piece]
-                ).astype(jnp.bfloat16)
-                out_copy(piece).start()
-
-        return carry
-
-    lax.fori_loop(0, chips, back, 0)
+    lax.fori_loop(0, chips + 5, turn, 0)
 
     def drain(step, carry):
         home = home_of(step)
-        pair_copy(step).wait_send()
         norm_copy(step).wait_send()
-        expert_copy(step).wait_send()
-        for piece in range(PIECES):
-
-            @pl.when(chip < chips - 1)
+        for piece in range(PIECES):
+            pair_copy(step, piece).wait_send()
+            expert_copy(step, piece).wait_send()
+
+            @pl.when(inner)
             def _():
-                right_copy(step, piece).wait_send()
-
-            @pl.when(chip > 0)
+                far_copy(step, piece).wait_send()
+                fall_copy(step, piece).wait_send()
+
+            @pl.when(jnp.logical_not(inner))
             def _():
-                left_copy(step, piece).wait_send()
-
-            @pl.when(chip < home)
+                near_copy(step, piece).wait_send()
+
+            @pl.when(inner & (home != chip))
             def _():
-                back_right_copy(step, piece).wait_send()
-
-            @pl.when(chip > home)
+                home_copy(step, piece, side).wait_send()
+
+            @pl.when(jnp.logical_not(inner) & (home != chip))
             def _():
-                back_left_copy(step, piece).wait_send()
+                back_copy(step, piece).wait_send()
 
         return carry
 
@@ -685,9 +687,6 @@
     features = heads * HEAD_SIZE
     hidden_units = gate_proj.shape[3]
     width = model // PIECES
-    query_rows = jnp.transpose(
-        queries[0].reshape(tokens, devices, heads, HEAD_SIZE), (1, 2, 0, 3)
-    ).reshape(devices, heads * tokens, HEAD_SIZE)
     labels = expert_labels[0]
     selected = jnp.sum(jnp.where(labels < local_experts, labels, 0), axis=1)
 
@@ -717,8 +716,7 @@
     result = pl.pallas_call(
         functools.partial(tick_kernel, sizes),
         out_shape=jax.ShapeDtypeStruct((tokens, model), bf16),
-        in_specs=[vmem, vmem, vmem, pl.BlockSpec(memory_space=pltpu.SMEM), vmem, vmem]
-        + [anywhere] * 5,
+        in_specs=[vmem, pl.BlockSpec(memory_space=pltpu.SMEM), vmem, vmem] + [anywhere] * 7,
         out_specs=vmem,
         scratch_shapes=[
             pltpu.VMEM((features, model), bf16),
@@ -726,7 +724,8 @@
             pltpu.VMEM((model, hidden_units), bf16),
             pltpu.VMEM((model, hidden_units), bf16),
             pltpu.VMEM((hidden_units, model), bf16),
-            pltpu.VMEM((devices, heads * tokens, HEAD_SIZE), bf16),
+            pltpu.VMEM((tokens, model), bf16),
+            pltpu.VMEM((devices, tokens, features), bf16),
             pltpu.VMEM((devices, message, HEAD_SIZE), bf16),
             pltpu.VMEM((total_rows, HEAD_SIZE), bf16),
             pltpu.VMEM((total_rows, HEAD_SIZE), bf16),
@@ -746,47 +745,48 @@
             pltpu.VMEM(block, f32),
             pltpu.VMEM(block, bf16),
             pltpu.VMEM(block, bf16),
-            pltpu.VMEM(block, bf16),
-            pltpu.VMEM(block, bf16),
+            pltpu.VMEM((2, PIECES, tokens, width), bf16),
             pltpu.VMEM((PIECES, tokens, width), bf16),
-            dma((5,)),
+            dma((6,)),
             dma((devices,)),
             dma((devices,)),
             dma((chips,)),
             dma((chips,)),
             dma((chips,)),
             dma((chips,)),
+            dma((2, chips, PIECES)),
+            dma((2, chips, PIECES)),
+            dma((2, chips, PIECES)),
+            dma((chips, PIECES)),
             dma((2, chips)),
             dma((2, chips, PIECES)),
             dma((2, chips, PIECES)),
-            dma((2, chips)),
-            dma((2, chips)),
-            dma((2, chips, PIECES)),
-            dma((2, chips, PIECES)),
+            dma((chips, PIECES)),
+            dma((2, PIECES)),
             dma((2, PIECES)),
         ],
         compiler_params=pltpu.CompilerParams(
             collective_id=0, has_side_effects=True, vmem_limit_bytes=60 * 2**20
         ),
     )(
-        query_rows,
         key_rows,
-        hidden[0],
         cache_fill,
         norm_gain,
         labels,
-        out_proj[0],
-        router_weight[0],
-        gate_proj[0, 0],
-        up_proj[0, 0],
-        down_proj[0, 0],
+        queries,
+        hidden,
+        out_proj,
+        router_weight,
+        gate_proj,
+        up_proj,
+        down_proj,
     )
     return result[None]
 
 
 def fits_one_kernel(mesh):
     devices = mesh.shape["expert"]
-    if devices % 2 or QUERY_HEADS % devices:
+    if devices != 2 * LINE or QUERY_HEADS % devices:
         return False
     return (QUERY_HEADS // KEY_VALUE_HEADS) % (2 * (QUERY_HEADS // devices)) == 0
 

time: 252 us -> 168 us (0.67)
  Pallas kernels: 244 us -> 161 us
    pallas_call x1, Pallas kernels: 244 us -> 161 us  [fused_shards(): pl.pallas_call(functools.partial(tick_kernel, sizes), out_shape=jax.Shape...]
where the time goes in v3:
time: 168 us; the launch traced here: 167 us
  Pallas kernels  161 us (96%)
  local copies, waits for them, and re-layouts  4.39 us (3%)
    pallas_call x1, Pallas kernels, fused_shards(): pl.pallas_call(functools.partial(tick_kernel, sizes), out_shape=jax.Shape...  161 us

profile of v3, /device:TPU:16, one launch (start us, length us, event | category | flops | bytes accessed | tf_op | source)
XLA Modules:
  0.0 167.3 jit_solution(330878447301740730)
XLA Ops:
  0.7 0.8 copy.15
  1.4 0.0 copy-start
  1.4 0.1 fusion
  1.5 0.1 pad.2.clone
  1.6 0.8 reshape_squeeze.7
  2.4 0.9 reshape_squeeze.6
  3.3 0.8 maximum_maximum_fusion.rows_ref
  4.1 0.0 copy-done
  4.1 161.4 %shard_map.118 = bf16[64,4096]{1,0:T(8,128)(2,1)} custom-call(bf16[2,256,128]{2,1,0:T(8,128)(2,1)} %maximum_maximum_fusion.rows_ref, s32[1]{0:T(128)S(6)} %copy.17.fill_ref, bf16[1,4096]{1,0:T(2,128)(2,1)} %gain_ref.1, s32[64,8]{1,0:T(8,128)} %bitcast.14, bf16[1,64,4096]{2,1,0:T(8,128)(2,1)} %query_hbm.1, bf16[1,64,4096]{2,1,0:T(8,128)(2,1)} %hidden_hbm.1, ...), custom_call_target="tpu_custom_call" | custom-call | tf_op jit(solution)/shard_map/pallas_call | solution.py:716
  165.4 1.9 %copy.18 = bf16[1,64,4096]{2,1,0:T(8,128)(2,1)} copy(bf16[1,64,4096]{2,1,0:T(8,128)(2,1)} %bitcast.13) | data formatting | bytes 1048576
  (3 shorter events, 0.0 us)
Async XLA Ops:
  1.4 2.6 %copy-start = (s32[1,64,8]{2,1,0:T(8,128)}, s32[1,64,8]{2,1,0:T(8,128)S(1)}, u32[]{:S(2)}) copy-start(s32[1,64,8]{2,1,0:T(8,128)S(1)} %copy.15) | copy-start | bytes 6148

commit v4 on v3

--- a/solution.py
+++ b/solution.py
@@ -189,14 +189,14 @@
     out_ref,
     out_proj_ref,
     router_ref,
-    gate_ref,
-    up_ref,
+    widen_ref,
     down_ref,
     hidden_ref,
     query_all,
     rows_all,
     keys_ref,
     values_ref,
+    relation_ref,
     attended_ref,
     pair_send,
     pair_recv,
@@ -248,6 +248,7 @@
     inner = (chip == 1) | (chip == 2)
     side = chip // 2
     features = query_all.shape[2]
+    units = down_ref.shape[0]
 
     def remote(source, target, send_sem, recv_sem, to, to_section=None):
         return pltpu.make_async_remote_copy(
@@ -265,8 +266,8 @@
             [
                 (out_proj_hbm.at[0], out_proj_ref),
                 (hidden_hbm.at[0], hidden_ref),
-                (gate_hbm.at[0, 0], gate_ref),
-                (up_hbm.at[0, 0], up_ref),
+                (gate_hbm.at[0, 0], widen_ref.at[:, :units]),
+                (up_hbm.at[0, 0], widen_ref.at[:, units:]),
                 (down_hbm.at[0, 0], down_ref),
                 (router_hbm.at[0], router_ref),
             ]
@@ -322,8 +323,11 @@
 
     for step in range(1, chips):
         rows_copy(step).start()
-    for step in range(1, devices):
-        query_copy(step).start()
+    def send_queries():
+        for step in range(1, devices):
+            query_copy(step).start()
+
+    pl.when(jnp.logical_not(inner))(send_queries)
     for copy in weights:
         copy.start()
     own_query.start()
@@ -339,15 +343,13 @@
         at = 0
         for ref in (keys_ref, values_ref):
             start = devices * cache_rows + device * tokens
-            ref[start : start + tokens] = rows_all[device, at : at + tokens]
+            ref[start : start + tokens, :HEAD_SIZE] = rows_all[device, at : at + tokens]
             at += tokens
         for ref in (keys_ref, values_ref):
             start = device * cache_rows
-            ref[start : start + cache_rows] = rows_all[device, at : at + cache_rows]
+            ref[start : start + cache_rows, :HEAD_SIZE] = rows_all[device, at : at + cache_rows]
             at += cache_rows
     own_query.wait()
-    for step in range(1, devices):
-        query_copy(step).wait_recv()
     for copy in weights[:2]:
         copy.wait()
 
@@ -357,6 +359,9 @@
     group_rows = heads * tokens
     column = lax.broadcasted_iota(jnp.int32, (group_rows, total_rows), 1)
     row_token = lax.broadcasted_iota(jnp.int32, (group_rows, total_rows), 0) % tokens
+    relation_ref[...] = jnp.where(column < cached, column, column - cached - row_token)
+    values_ref[:, HEAD_SIZE:] = jnp.ones((total_rows, HEAD_SIZE), jnp.bfloat16)
+    first_row = lax.broadcasted_iota(jnp.int32, (1, total_rows), 1)
 
     def home_of(step):
         return jnp.where(step % 2 == 0, step // 2, chips - 1 - step // 2)
@@ -403,12 +408,12 @@
             2 * home_of(step) + core,
         )
 
-    def norm_copy(step):
+    def norm_copy(step, piece):
         return remote(
-            normed_ref.at[step, 0],
-            normed_ref.at[step, 1],
-            norm_sem.at[0, step],
-            norm_sem.at[1, step],
+            normed_ref.at[step, piece, pl.ds(0, tokens)],
+            normed_ref.at[step, piece, pl.ds(tokens, tokens)],
+            norm_sem.at[0, step, piece],
+            norm_sem.at[1, step, piece],
             partner,
         )
 
@@ -426,33 +431,32 @@
         home = home_of(step)
         for which in range(2):
             owner = 2 * home + (core if which == 0 else 1 - core)
-            scores = (
-                lax.dot_general(
-                    jnp.concatenate(
-                        [
-                            query_all[owner, :, head * HEAD_SIZE : (head + 1) * HEAD_SIZE]
-                            for head in range(heads)
-                        ],
-                        axis=0,
-                    ),
-                    keys_ref[...],
-                    (((1,), (1,)), ((), ())),
-                    preferred_element_type=jnp.float32,
-                )
-                * (1.0 / math.sqrt(HEAD_SIZE))
+            @pl.when(owner != me)
+            def _():
+                query_copy((me + devices - owner) % devices).wait_recv()
+
+            scores = lax.dot_general(
+                jnp.concatenate(
+                    [
+                        query_all[owner, :, head * HEAD_SIZE : (head + 1) * HEAD_SIZE]
+                        for head in range(heads)
+                    ],
+                    axis=0,
+                ),
+                keys_ref[...],
+                (((1,), (1,)), ((), ())),
+                preferred_element_type=jnp.float32,
             )
-            limit = jnp.where(column < cached, fill, cached + owner * tokens + row_token + 1)
-            visible = column < limit
-            masked = jnp.where(visible, scores, -1e30)
+            limit = jnp.where(first_row < cached, fill, owner * tokens + 1)
+            masked = jnp.where(relation_ref[...] < limit, scores, -1e30)
             highest = jnp.max(masked, axis=1, keepdims=True)
-            weight = jnp.where(visible, jnp.exp(masked - highest), 0.0)
-            totals = jnp.sum(weight, axis=1, keepdims=True)
-            mean = (
-                jnp.dot(
-                    weight.astype(jnp.bfloat16), values_ref[...], preferred_element_type=jnp.float32
-                )
-                / totals
-            ).astype(jnp.bfloat16)
+            weight = jnp.exp2(
+                (masked - highest) * (1.0 / (math.sqrt(HEAD_SIZE) * math.log(2.0)))
+            )
+            summed = jnp.dot(
+                weight.astype(jnp.bfloat16), values_ref[...], preferred_element_type=jnp.float32
+            )
+            mean = (summed[:, :HEAD_SIZE] / summed[:, HEAD_SIZE:]).astype(jnp.bfloat16)
             for head in range(heads):
                 attended_ref[
                     which * tokens : (which + 1) * tokens, head * HEAD_SIZE : (head + 1) * HEAD_SIZE
@@ -519,18 +523,22 @@
         inverse = lax.rsqrt(squares / (PIECES * width) + 1e-06)
         for piece in range(PIECES):
             columns = slice(piece * width, (piece + 1) * width)
-            normed_ref[step, 0, :, columns] = (
+            normed_ref[step, piece, :tokens] = (
                 part_ref[step, piece] * inverse * gain_ref[:, columns].astype(jnp.float32)
             ).astype(jnp.bfloat16)
-        norm_copy(step).start()
+            norm_copy(step, piece).start()
 
         @pl.when(home == chip)
         def _():
             for piece in range(PIECES):
                 mixed_ref[piece] = part_ref[step, piece]
-            logits = jnp.dot(
-                normed_ref[step, 0], router_ref[...], preferred_element_type=jnp.float32
-            )
+            logits = jnp.zeros((tokens, router_ref.shape[1]), jnp.float32)
+            for piece in range(PIECES):
+                logits += jnp.dot(
+                    normed_ref[step, piece, :tokens],
+                    router_ref[piece * width : (piece + 1) * width],
+                    preferred_element_type=jnp.float32,
+                )
             labels = label_ref[...]
             expert_at = lax.broadcasted_iota(jnp.int32, logits.shape, 1)
             picked = []
@@ -548,10 +556,15 @@
                 chosen += jnp.where(labels[:, at : at + 1] < local_experts, weight, 0.0)
             combine_ref[...] = jnp.broadcast_to(chosen / total, combine_ref.shape)
 
-        norm_copy(step).wait_recv()
-        rows = normed_ref[step].reshape(2 * tokens, PIECES * width)
-        gated = jnp.dot(rows, gate_ref[...], preferred_element_type=jnp.float32)
-        lifted = jnp.dot(rows, up_ref[...], preferred_element_type=jnp.float32)
+        widened = jnp.zeros((2 * tokens, 2 * units), jnp.float32)
+        for piece in range(PIECES):
+            norm_copy(step, piece).wait_recv()
+            widened += jnp.dot(
+                normed_ref[step, piece],
+                widen_ref[piece * width : (piece + 1) * width],
+                preferred_element_type=jnp.float32,
+            )
+        gated, lifted = widened[:, :units], widened[:, units:]
         activation = gated / (1.0 + jnp.exp(-gated)) * lifted
         selected = jnp.concatenate(
             [
@@ -615,6 +628,7 @@
 
     def turn(time, carry):
         pl.when(within(time))(lambda: project(time))
+        pl.when((time == 0) & inner)(send_queries)
         pl.when(within(time - 1) & inner)(lambda: forward(time - 1))
         pl.when(within(time - 4) & inner)(lambda: fold(time - 4))
         layer_step = time - jnp.where(inner, 2, 3)
@@ -627,8 +641,8 @@
 
     def drain(step, carry):
         home = home_of(step)
-        norm_copy(step).wait_send()
-        for piece in range(PIECES):
+        for piece in range(PIECES):
+            norm_copy(step, piece).wait_send()
             pair_copy(step, piece).wait_send()
             expert_copy(step, piece).wait_send()
 
@@ -721,14 +735,14 @@
         scratch_shapes=[
             pltpu.VMEM((features, model), bf16),
             pltpu.VMEM(router_weight.shape[1:], bf16),
-            pltpu.VMEM((model, hidden_units), bf16),
-            pltpu.VMEM((model, hidden_units), bf16),
+            pltpu.VMEM((model, 2 * hidden_units), bf16),
             pltpu.VMEM((hidden_units, model), bf16),
             pltpu.VMEM((tokens, model), bf16),
             pltpu.VMEM((devices, tokens, features), bf16),
             pltpu.VMEM((devices, message, HEAD_SIZE), bf16),
             pltpu.VMEM((total_rows, HEAD_SIZE), bf16),
-            pltpu.VMEM((total_rows, HEAD_SIZE), bf16),
+            pltpu.VMEM((total_rows, 2 * HEAD_SIZE), bf16),
+            pltpu.VMEM((heads * tokens, total_rows), jnp.int32),
             pltpu.VMEM((2 * tokens, features), bf16),
             pltpu.VMEM(block, bf16),
             pltpu.VMEM(block, bf16),
@@ -737,7 +751,7 @@
             pltpu.VMEM(block, bf16),
             pltpu.VMEM(block, bf16),
             pltpu.VMEM(block, bf16),
-            pltpu.VMEM((chips, 2, tokens, model), bf16),
+            pltpu.VMEM((chips, PIECES, 2 * tokens, width), bf16),
             pltpu.VMEM((PIECES, tokens, width), f32),
             pltpu.VMEM((tokens, 128), f32),
             pltpu.VMEM(block, bf16),
@@ -758,7 +772,7 @@
             dma((2, chips, PIECES)),
             dma((2, chips, PIECES)),
             dma((chips, PIECES)),
-            dma((2, chips)),
+            dma((2, chips, PIECES)),
             dma((2, chips, PIECES)),
             dma((2, chips, PIECES)),
             dma((chips, PIECES)),

time: 168 us -> 163 us (0.970)
  Pallas kernels: 161 us -> 157 us
    pallas_call x1, Pallas kernels: 161 us -> 157 us  [fused_shards(): pl.pallas_call(functools.partial(tick_kernel, sizes), out_shape=jax.Shape...]
where the time goes in v4:
time: 163 us
  Pallas kernels  157 us (96%)
  local copies, waits for them, and re-layouts  4.39 us (3%)
    pallas_call x1, Pallas kernels, fused_shards(): pl.pallas_call(functools.partial(tick_kernel, sizes), out_shape=jax.Shape...  157 us

profile of v4, /device:TPU:16, one launch (start us, length us, event | category | flops | bytes accessed | tf_op | source)
XLA Modules:
  0.0 162.9 jit_solution(3540683521702747938)
XLA Ops:
  0.7 0.8 copy.15
  1.4 0.0 copy-start
  1.4 0.1 fusion
  1.5 0.1 pad.2.clone
  1.6 0.8 reshape_squeeze.7
  2.4 0.9 reshape_squeeze.6
  3.3 0.8 maximum_maximum_fusion.rows_ref
  4.1 0.0 copy-done
  4.1 157.0 %shard_map.118 = bf16[64,4096]{1,0:T(8,128)(2,1)} custom-call(bf16[2,256,128]{2,1,0:T(8,128)(2,1)} %maximum_maximum_fusion.rows_ref, s32[1]{0:T(128)S(6)} %copy.17.fill_ref, bf16[1,4096]{1,0:T(2,128)(2,1)} %gain_ref.1, s32[64,8]{1,0:T(8,128)} %bitcast.14, bf16[1,64,4096]{2,1,0:T(8,128)(2,1)} %query_hbm.1, bf16[1,64,4096]{2,1,0:T(8,128)(2,1)} %hidden_hbm.1, ...), custom_call_target="tpu_custom_call" | custom-call | tf_op jit(solution)/shard_map/pallas_call | solution.py:730
  161.1 1.9 %copy.18 = bf16[1,64,4096]{2,1,0:T(8,128)(2,1)} copy(bf16[1,64,4096]{2,1,0:T(8,128)(2,1)} %bitcast.13) | data formatting | bytes 1048576
  (3 shorter events, 0.0 us)
Async XLA Ops:
  1.4 2.6 %copy-start = (s32[1,64,8]{2,1,0:T(8,128)}, s32[1,64,8]{2,1,0:T(8,128)S(1)}, u32[]{:S(2)}) copy-start(s32[1,64,8]{2,1,0:T(8,128)S(1)} %copy.15) | copy-start | bytes 6148

commit v5 on v4

--- a/solution.py
+++ b/solution.py
@@ -274,6 +274,18 @@
         )
     ]
 
+    def key_head(chip_at):
+        return (chip_at * 2 * heads) // head_group
+
+    def query_part(to):
+        return query_hbm.at[0, :, pl.ds(pl.multiple_of(to * features, HEAD_SIZE), features)]
+
+    own_query = pltpu.make_async_copy(query_part(me), query_all.at[me], query_recv_sem.at[0])
+
+    for copy in weights:
+        copy.start()
+    own_query.start()
+    rows_all[me] = rows_ref[key_head(chip)]
     barrier = pltpu.get_barrier_semaphore()
     for step in range(1, devices):
         pl.semaphore_signal(
@@ -282,12 +294,6 @@
     pl.semaphore_signal(barrier, inc=1, device_id=(next_section, me), device_id_type=MESH)
     pl.semaphore_signal(barrier, inc=1, device_id=(before_section, me), device_id_type=MESH)
     pl.semaphore_wait(barrier, devices + 1)
-
-    def key_head(chip_at):
-        return (chip_at * 2 * heads) // head_group
-
-    def query_part(to):
-        return query_hbm.at[0, :, pl.ds(pl.multiple_of(to * features, HEAD_SIZE), features)]
 
     def query_copy(step):
         to = (me + step) % devices
@@ -299,8 +305,6 @@
             to,
         )
 
-    own_query = pltpu.make_async_copy(query_part(me), query_all.at[me], query_recv_sem.at[0])
-
     def rows_copy(step):
         to_chip = (chip + step) % chips
         return remote(
@@ -328,10 +332,6 @@
             query_copy(step).start()
 
     pl.when(jnp.logical_not(inner))(send_queries)
-    for copy in weights:
-        copy.start()
-    own_query.start()
-    rows_all[me] = rows_ref[key_head(chip)]
     for step in range(chips):
         if step > 0:
             rows_copy(step).wait_recv()
@@ -461,6 +461,21 @@
                 attended_ref[
                     which * tokens : (which + 1) * tokens, head * HEAD_SIZE : (head + 1) * HEAD_SIZE
                 ] = mean[head * tokens : (head + 1) * tokens]
+        def ship(piece):
+            @pl.when(home == chip)
+            def _():
+                part_ref[step, piece] += hidden_ref[
+                    :, piece * width : (piece + 1) * width
+                ].astype(jnp.float32)
+
+            pair_copy(step, piece).wait_recv()
+            part_ref[step, piece] += pair_recv[step, piece].astype(jnp.float32)
+
+            @pl.when(jnp.logical_not(inner))
+            def _():
+                inward_send[step, piece] = part_ref[step, piece].astype(jnp.bfloat16)
+                near_copy(step, piece).start()
+
         for piece in range(PIECES):
             product = jnp.dot(
                 attended_ref[...],
@@ -470,30 +485,23 @@
             part_ref[step, piece] = product[:tokens]
             pair_send[step, piece] = product[tokens:].astype(jnp.bfloat16)
             pair_copy(step, piece).start()
-
-        @pl.when(home == chip)
-        def _():
-            for piece in range(PIECES):
-                part_ref[step, piece] += hidden_ref[
-                    :, piece * width : (piece + 1) * width
-                ].astype(jnp.float32)
-
-        for piece in range(PIECES):
-            pair_copy(step, piece).wait_recv()
-            part_ref[step, piece] += pair_recv[step, piece].astype(jnp.float32)
-
-            @pl.when(jnp.logical_not(inner))
-            def _():
-                inward_send[step, piece] = part_ref[step, piece].astype(jnp.bfloat16)
-                near_copy(step, piece).start()
-
-    def forward(step):
-        for piece in range(PIECES):
-            near_copy(step, piece).wait_recv()
-            inward_send[step, piece] = (
-                part_ref[step, piece] + near_recv[step, piece].astype(jnp.float32)
-            ).astype(jnp.bfloat16)
-            far_copy(step, piece).start()
+            if piece > 0:
+                ship(piece - 1)
+        ship(PIECES - 1)
+
+    def within(step):
+        return (step >= 0) & (step < chips)
+
+    def forward(step, piece):
+        near_copy(step, piece).wait_recv()
+        inward_send[step, piece] = (
+            part_ref[step, piece] + near_recv[step, piece].astype(jnp.float32)
+        ).astype(jnp.bfloat16)
+        far_copy(step, piece).start()
+
+    def forward_first():
+        for piece in range(PIECES):
+            forward(0, piece)
 
     my_expert = (me // SPLIT).astype(jnp.float32)
     select_at = 2 * tokens + 2 * cache_rows
@@ -564,6 +572,7 @@
                 widen_ref[piece * width : (piece + 1) * width],
                 preferred_element_type=jnp.float32,
             )
+            pl.when(inner & within(step + 1))(functools.partial(forward, step + 1, piece))
         gated, lifted = widened[:, :units], widened[:, units:]
         activation = gated / (1.0 + jnp.exp(-gated)) * lifted
         selected = jnp.concatenate(
@@ -623,21 +632,18 @@
             ).astype(jnp.bfloat16)
             out_copy(piece).start()
 
-    def within(step):
-        return (step >= 0) & (step < chips)
-
     def turn(time, carry):
         pl.when(within(time))(lambda: project(time))
         pl.when((time == 0) & inner)(send_queries)
-        pl.when(within(time - 1) & inner)(lambda: forward(time - 1))
+        pl.when((time == 0) & inner)(forward_first)
+        layer_step = time - jnp.where(inner, 1, 3)
+        pl.when(within(layer_step))(lambda: layer(layer_step))
         pl.when(within(time - 4) & inner)(lambda: fold(time - 4))
-        layer_step = time - jnp.where(inner, 2, 3)
-        pl.when(within(layer_step))(lambda: layer(layer_step))
-        ending = time - 5
+        ending = time - 6
         pl.when(within(ending) & (home_of(ending) == chip))(lambda: finish(ending))
         return carry
 
-    lax.fori_loop(0, chips + 5, turn, 0)
+    lax.fori_loop(0, chips + 6, turn, 0)
 
     def drain(step, carry):
         home = home_of(step)

time: 163 us -> 133 us (0.82); the launches traced: 163 us -> 130 us
  Pallas kernels: 157 us -> 125 us
    pallas_call x1, Pallas kernels: 157 us -> 125 us  [fused_shards(): pl.pallas_call(functools.partial(tick_kernel, sizes), out_shape=jax.Shape...]
where the time goes in v5:
time: 133 us; the launch traced here: 130 us
  Pallas kernels  125 us (94%)
  local copies, waits for them, and re-layouts  4.39 us (3%)
    pallas_call x1, Pallas kernels, fused_shards(): pl.pallas_call(functools.partial(tick_kernel, sizes), out_shape=jax.Shape...  125 us

profile of v5, /device:TPU:16, one launch (start us, length us, event | category | flops | bytes accessed | tf_op | source)
XLA Modules:
  0.0 130.5 jit_solution(8079754396388065736)
XLA Ops:
  0.7 0.8 copy.15
  1.4 0.0 copy-start
  1.4 0.1 fusion
  1.5 0.1 pad.2.clone
  1.6 0.8 reshape_squeeze.7
  2.4 0.9 reshape_squeeze.6
  3.3 0.8 maximum_maximum_fusion.rows_ref
  4.1 0.0 copy-done
  4.1 124.5 %shard_map.118 = bf16[64,4096]{1,0:T(8,128)(2,1)} custom-call(bf16[2,256,128]{2,1,0:T(8,128)(2,1)} %maximum_maximum_fusion.rows_ref, s32[1]{0:T(128)S(6)} %copy.17.fill_ref, bf16[1,4096]{1,0:T(2,128)(2,1)} %gain_ref.1, s32[64,8]{1,0:T(8,128)} %bitcast.14, bf16[1,64,4096]{2,1,0:T(8,128)(2,1)} %query_hbm.1, bf16[1,64,4096]{2,1,0:T(8,128)(2,1)} %hidden_hbm.1, ...), custom_call_target="tpu_custom_call" | custom-call | tf_op jit(solution)/shard_map/pallas_call | solution.py:736
  128.6 1.9 %copy.18 = bf16[1,64,4096]{2,1,0:T(8,128)(2,1)} copy(bf16[1,64,4096]{2,1,0:T(8,128)(2,1)} %bitcast.13) | data formatting | bytes 1048576
  (3 shorter events, 0.0 us)
Async XLA Ops:
  1.4 2.6 %copy-start = (s32[1,64,8]{2,1,0:T(8,128)}, s32[1,64,8]{2,1,0:T(8,128)S(1)}, u32[]{:S(2)}) copy-start(s32[1,64,8]{2,1,0:T(8,128)S(1)} %copy.15) | copy-start | bytes 6148

commit v6 on v5

--- a/solution.py
+++ b/solution.py
@@ -169,7 +169,7 @@
 
 
 MESH = pl.DeviceIdType.MESH
-PIECES = 4
+PIECES = 8
 LINE = 4
 
 

time: 133 us -> 151 us (1.14)
  the two profiles are of different devices: /device:TPU:16 before, /device:TPU:8 now
where the time goes in v6:
time: 151 us
  Pallas kernels  145 us (96%)
  local copies, waits for them, and re-layouts  4.39 us (3%)
    pallas_call x1, Pallas kernels, fused_shards(): pl.pallas_call(functools.partial(tick_kernel, sizes), out_shape=jax.Shape...  145 us

profile of v6, /device:TPU:8, one launch (start us, length us, event | category | flops | bytes accessed | tf_op | source)
XLA Modules:
  0.0 150.7 jit_solution(15593170653729455208)
XLA Ops:
  0.7 0.8 copy.15
  1.4 0.0 copy-start
  1.4 0.1 fusion
  1.5 0.1 pad.2.clone
  1.6 0.8 reshape_squeeze.7
  2.4 0.9 reshape_squeeze.6
  3.3 0.8 maximum_maximum_fusion.rows_ref
  4.1 0.0 copy-done
  4.1 144.8 %shard_map.118 = bf16[64,4096]{1,0:T(8,128)(2,1)} custom-call(bf16[2,256,128]{2,1,0:T(8,128)(2,1)} %maximum_maximum_fusion.rows_ref, s32[1]{0:T(128)S(6)} %copy.17.fill_ref, bf16[1,4096]{1,0:T(2,128)(2,1)} %gain_ref.1, s32[64,8]{1,0:T(8,128)} %bitcast.14, bf16[1,64,4096]{2,1,0:T(8,128)(2,1)} %query_hbm.1, bf16[1,64,4096]{2,1,0:T(8,128)(2,1)} %hidden_hbm.1, ...), custom_call_target="tpu_custom_call" | custom-call | tf_op jit(solution)/shard_map/pallas_call | solution.py:736
  148.9 1.9 %copy.18 = bf16[1,64,4096]{2,1,0:T(8,128)(2,1)} copy(bf16[1,64,4096]{2,1,0:T(8,128)(2,1)} %bitcast.13) | data formatting | bytes 1048576
  (3 shorter events, 0.0 us)
Async XLA Ops:
  1.4 2.6 %copy-start = (s32[1,64,8]{2,1,0:T(8,128)}, s32[1,64,8]{2,1,0:T(8,128)S(1)}, u32[]{:S(2)}) copy-start(s32[1,64,8]{2,1,0:T(8,128)S(1)} %copy.15) | copy-start | bytes 6148
